TPU v7x, 128 devices: a whole 4x4x4 slice. The times are simulated.
128 devices in a mesh: dp: 8 (over x_lo, y), tensor: 16 (over x_hi, z, core).
Axes of the slice: x: 4 (x_hi: 2, x_lo: 2; x = x_hi * 2 + x_lo), y: 4, z: 4, core: 2. Of those that a mesh axis runs over, the one named last changes fastest.
Arguments:
- hidden: bfloat16 [8, 512, 8192], P('dp'), may hold values from -70 to 70, as said below
- lengths: int32 [8], P('dp'), may hold values from 128 to 512, as said below
- norm_gain: float32 [8192], replicated, may hold values from 0.1 to 1.9
- w_q: float32 [8192, 8192], P(('dp', 'tensor')), may hold values from -1 to 1
- w_k: float32 [8192, 1024], P(('dp', 'tensor')), may hold values from -1 to 1
- w_v: float32 [8192, 1024], P(('dp', 'tensor')), may hold values from -1 to 1
- w_out: float32 [8192, 8192], P(('dp', 'tensor')), may hold values from -1 to 1
- b_q: float32 [8192], replicated, may hold values from -20 to 20
- b_k: float32 [1024], replicated, may hold values from -20 to 20
- b_v: float32 [1024], replicated, may hold values from -4 to 4
Outputs:
- layer_out: bfloat16 [8, 512, 8192], P('dp')
Inputs may be any that keep to these rules, and one draw needn't show every extreme that they name: `hidden`: activations have row scales between 1 and 10. `lengths`: at least one replica has all 512 tokens live in every draw.
All inputs are finite; a program needn't handle non-finite values.
Results may differ from a plain program's by a relative error of at most 0.023.
Values may be sent and summed in bfloat16 or wider, within the bound.
A program may use at most 256 MiB of HBM per device.

v0:
```python
import jax
import jax.numpy as jnp
from jax import lax
from jax.sharding import PartitionSpec as P

HQ = 64
KV = 8
HD = 128
TILE = 128


THETA = 1000000.0
NORM_EPS = 1e-06
PEAK_EPS = 1e-06
LEVEL_TOP = 127.0


def tile_peaks(block):
    rows, cols = block.shape
    mags = jnp.abs(block).reshape(rows // TILE, TILE, cols // TILE, TILE)
    return jnp.max(mags, axis=(1, 3))


def quantize(block, scales):
    rows, cols = block.shape
    count, tiles = scales.shape
    shaped = block.reshape(count, rows // count, tiles, cols // tiles)
    return (
        jnp.floor(shaped / scales.astype(jnp.float32)[:, None, :, None] + 0.5)
        .astype(jnp.bfloat16)
        .reshape(rows, cols)
    )


def dequantize(levels, scales):
    rows, cols = levels.shape
    count, tiles = scales.shape
    shaped = levels.reshape(count, rows // count, tiles, cols // tiles).astype(jnp.float32)
    return (
        (shaped * scales.astype(jnp.float32)[:, None, :, None])
        .astype(jnp.bfloat16)
        .reshape(rows, cols)
    )


def rotary(values, count, tokens):
    positions = jnp.arange(tokens).astype(jnp.float32)
    freqs = THETA ** (-jnp.arange(0, HD, 2).astype(jnp.float32) / HD)
    angles = positions[:, None] * freqs[None, :]
    cosine = jnp.cos(angles)[:, None, :]
    sine = jnp.sin(angles)[:, None, :]
    shaped = values.reshape(tokens, count, HD)
    first = shaped[:, :, : HD // 2]
    second = shaped[:, :, HD // 2 :]
    return jnp.concatenate((first * cosine - second * sine, second * cosine + first * sine), axis=2)


def attention(query, keys, values, length, heads, kv_heads):
    tokens = query.shape[0]
    group = heads // kv_heads
    grouped = query.reshape(tokens, kv_heads, group, HD)
    scores = jnp.einsum(
        "qkgd,skd->kgqs", grouped, keys, preferred_element_type=jnp.float32
    ) * HD ** (-0.5)
    rows = jnp.arange(tokens)[:, None]
    cols = jnp.arange(tokens)[None, :]
    keep = (cols <= rows) & (cols < length)
    scores = jnp.where(keep[None, None], scores, -1e30)
    peak = jnp.max(scores, axis=3, keepdims=True)
    expo = jnp.exp(scores - peak)
    probs = (expo / jnp.sum(expo, axis=3, keepdims=True)).astype(jnp.bfloat16)
    mixed = jnp.einsum("kgqs,skd->qkgd", probs, values, preferred_element_type=jnp.float32)
    return mixed.astype(jnp.bfloat16).reshape(tokens, heads * HD)


def local(hidden, lengths, norm_gain, w_q, w_k, w_v, w_out, b_q, b_k, b_v):
    tensor_size = lax.axis_size("tensor")
    rank = lax.axis_index("tensor")
    rows_dev = w_q.shape[0]
    head_cols = w_q.shape[1] // tensor_size
    repeat = max(1, tensor_size // KV)
    kv_cols = KV * repeat * HD // tensor_size
    heads_here = HQ // tensor_size
    kv_here = kv_cols // HD
    proj_cols = head_cols + 2 * kv_cols

    def columns(weight, copies):
        if copies > 1:
            weight = jnp.repeat(weight.reshape(rows_dev, -1, HD), copies, axis=1)
        return weight.reshape(rows_dev, tensor_size, -1)

    outgoing = jnp.concatenate(
        (columns(w_q, 1), columns(w_k, repeat), columns(w_v, repeat), columns(w_out, 1)), axis=2
    )
    width = outgoing.shape[2]
    arrived = lax.all_to_all(outgoing, "tensor", split_axis=1, concat_axis=0, tiled=True).reshape(
        -1, width
    )
    scales = ((tile_peaks(arrived) + PEAK_EPS) / LEVEL_TOP).astype(jnp.bfloat16)
    levels = quantize(arrived, scales)
    local_hidden = hidden[0]
    tokens = local_hidden.shape[0]
    wide = local_hidden.astype(jnp.float32)
    normed = (
        wide * lax.rsqrt(jnp.mean(wide * wide, axis=1, keepdims=True) + NORM_EPS) * norm_gain
    ).astype(jnp.bfloat16)
    levels, scales = (
        lax.all_gather(levels, "dp", axis=0, tiled=True),
        lax.all_gather(scales, "dp", axis=0, tiled=True),
    )
    own_rows = dequantize(levels, scales)
    projected = jnp.dot(normed, own_rows[:, :proj_cols], preferred_element_type=jnp.float32)
    bias_q = lax.dynamic_slice_in_dim(b_q, rank * head_cols, head_cols)
    kv_start = rank * heads_here // (HQ // KV) * HD
    bias_k = lax.dynamic_slice_in_dim(b_k, kv_start, kv_cols)
    bias_v = lax.dynamic_slice_in_dim(b_v, kv_start, kv_cols)
    query = rotary(projected[:, :head_cols] + bias_q, heads_here, tokens).astype(jnp.bfloat16)
    keys = rotary(projected[:, head_cols : head_cols + kv_cols] + bias_k, kv_here, tokens).astype(
        jnp.bfloat16
    )
    values = (
        (projected[:, head_cols + kv_cols :] + bias_v)
        .reshape(tokens, kv_here, HD)
        .astype(jnp.bfloat16)
    )
    attended = attention(query, keys, values, lengths[0], heads_here, kv_here)
    out_rows = own_rows[:, proj_cols:]
    partial_value = lax.dot_general(
        attended, out_rows, (((1,), (1,)), ((), ())), preferred_element_type=jnp.float32
    )
    total = lax.psum(partial_value.astype(jnp.bfloat16), "tensor")
    return total[None]


def solution(mesh):
    placed = (
        P("dp", None, None),
        P("dp"),
        P(),
        P(("dp", "tensor"), None),
        P(("dp", "tensor"), None),
        P(("dp", "tensor"), None),
        P(("dp", "tensor"), None),
        P(),
        P(),
        P(),
    )
    return jax.shard_map(
        local, mesh=mesh, in_specs=placed, out_specs=P("dp", None, None), check_vma=False
    )
```

profile of v0, /device:TPU:27, one launch (start us, length us, event | category | flops | bytes accessed | tf_op | source)
XLA Modules:
  0.0 549.0 jit_solution(6583226158215299613)
XLA Ops:
  6.5 0.0 copy-start.1
  6.5 0.0 all-gather.2.cloned.1.call-start
  6.5 2.9 copy.56
  9.5 1.0 copy.55
  10.5 1.0 copy.54
  11.5 0.0 copy-done.1
  11.5 1.2 copy.53
  12.7 0.2 broadcast_in_dim.15
  12.9 0.2 broadcast_in_dim.14
  13.1 0.5 pad_maximum_fusion
  13.6 3.0 copy.39
  16.7 69.2 %all_to_all.15 = f32[64,16,1280]{2,0,1:T(8,128)S(1)} all-to-all(f32[64,16,1280]{2,0,1:T(8,128)S(1)} %copy.39), channel_id=1, replica_groups=mesh['dp'=8,'tensor'=16] {'tensor'}, dimensions={1} | all-to-all | bytes 10485760 | tf_op jit(solution)/shard_map/all_to_all | solution.py:96
  85.9 0.0 copy-start
  85.9 2.3 copy-done
  88.2 0.5 fusion.14
  88.7 0.1 reduce_max.27
  88.8 0.1 copy.40
  88.9 0.4 div.61
  89.3 3.6 copy.66
  93.0 5.9 %copy.41 = f32[1024,1280]{1,0:T(8,128)} copy(f32[1024,1280]{0,1:T(8,128)} %bitcast.93) | data formatting | bytes 10485760 | tf_op jit(solution)/shard_map/div | solution.py:29
  98.9 6.5 %fusion.13 = bf16[1024,1280]{1,0:T(8,128)(2,1)} fusion(f32[1024,1280]{1,0:T(8,128)} %copy.41, f32[64,16,1280]{2,0,1:T(8,128)} %copy-done), kind=kLoop, calls=%fused_computation.20 | loop fusion | flops 5242880 | bytes 13107200 | tf_op jit(solution)/shard_map/convert_element_type | solution.py:30
  105.3 0.0 all-gather.2.cloned.1.call-update
  105.4 0.2 all-reduce.2.cloned.1.call-start
  106.3 0.8 dynamic_slice.10
  107.0 0.8 dynamic_slice.9
  107.8 0.8 dynamic_slice.11
  108.6 5.1 fusion
  113.7 0.1 fusion.23
  113.8 1.0 multiply_cosine_fusion
  114.8 20.7 %all_gather.7 = bf16[64,10]{1,0:T(8,128)(2,1)S(1)} all-gather(bf16[8,10]{1,0:T(8,128)(2,1)S(1)} %multiply_convert_fusion.1), channel_id=1, replica_groups=mesh['dp'=8,'tensor'=16] {'dp'}, dimensions={0}, use_global_device_ids=true | all-gather | bytes 1440 | tf_op jit(solution)/shard_map/all_gather | solution.py:109
  135.6 0.1 copy.42
  135.6 13.8 %mul.197 = f32[64,128,10,128]{1,0,3,2:T(8,128)} broadcast(bf16[64,10]{0,1:T(8,128)(2,1)S(1)} %copy.42), dimensions={0,2} | broadcast | bytes 41944320 | tf_op jit(solution)/shard_map/mul | solution.py:40
  149.5 44.2 %copy.65 = f32[160,8,64,128]{3,1,2,0:T(8,128)} copy(f32[160,8,64,128]{3,2,1,0:T(8,128)} %bitcast.90) | data formatting | bytes 83886080
  193.7 43.0 %copy.43 = f32[8192,1280]{1,0:T(8,128)} copy(f32[8192,1280]{0,1:T(8,128)} %bitcast.91) | data formatting | bytes 83886080 | tf_op jit(solution)/shard_map/mul | solution.py:40
  236.7 0.0 copy-start.3
  236.7 74.6 %all-gather.2.cloned.1.call-done = bf16[8192,1280]{1,0:T(8,128)(2,1)} async-done(((bf16[1024,1280]{1,0:T(8,128)(2,1)}), bf16[8192,1280]{1,0:T(8,128)(2,1)}) %all-gather.2.cloned.1.call-update) | async-done | bytes 20971536 | tf_op jit(solution)/shard_map/all_gather | solution.py:108
  311.2 27.9 %multiply_convert_fusion = bf16[8192,1280]{1,0:T(8,128)(2,1)} fusion(f32[8192,1280]{1,0:T(8,128)} %copy.43, bf16[8192,1280]{1,0:T(8,128)(2,1)} %all-gather.2.cloned.1.call-done), kind=kLoop, calls=%fused_computation.1 | loop fusion | flops 31457280 | bytes 83886080 | tf_op jit(solution)/shard_map/convert_element_type | solution.py:41
  339.2 0.0 copy-done.3
  339.2 12.0 %fusion.3 = f32[512,768]{1,0:T(8,128)S(1)} fusion(bf16[8192,1280]{1,0:T(8,128)(2,1)} %multiply_convert_fusion, bf16[1,512,8192]{2,1,0:T(8,128)(2,1)} %param.10, f32[8192]{0:T(1024)S(1)} %copy-done.3, f32[512]{0:T(512)S(1)} %add_rsqrt_fusion), kind=kOutput, calls=%fused_computation.7 | convolution fusion | flops 6459228160 | bytes 22579200 | tf_op jit(solution)/shard_map/dot_general | solution.py:112
  351.2 0.0 copy-start.2
  351.2 1.1 copy-done.2
  352.4 0.1 slice_add_fusion
  352.5 0.4 reshape.250
  352.9 0.6 fusion.48
  353.5 1.0 fusion.36
  354.4 1.4 fusion.44
  355.9 0.3 subtract_convert_fusion
  356.2 1.2 fusion.16
  357.4 0.9 fusion.15
  358.3 2.4 fusion.20
  360.7 10.3 %fusion.5 = bf16[1,512,8192]{2,1,0:T(8,128)(2,1)} fusion(bf16[512,512]{0,1:T(8,128)(2,1)S(1)} %bitcast.104, bf16[8192,1280]{1,0:T(8,128)(2,1)} %multiply_convert_fusion), kind=kOutput, calls=%fused_computation.10 | convolution fusion | flops 4299161600 | bytes 17301504 | tf_op jit(solution)/shard_map/dot_general | solution.py:128
  371.1 0.0 all-reduce.2.cloned.1.call-update
  371.1 163.3 %all-reduce.2.cloned.1.call-done = bf16[1,512,8192]{2,1,0:T(8,128)(2,1)} async-done(((bf16[1,512,8192]{2,1,0:T(8,128)(2,1)}), bf16[1,512,8192]{2,1,0:T(8,128)(2,1)}) %all-reduce.2.cloned.1.call-update) | async-done | bytes 8388624 | tf_op jit(solution)/shard_map/psum | solution.py:131
  534.3 7.8 %copy.69 = bf16[1,512,8192]{2,1,0:T(8,128)(2,1)} copy(bf16[1,512,8192]{2,1,0:T(8,128)(2,1)} %all-reduce.2.cloned.1.call-done) | data formatting | bytes 16777216
  (6 shorter events, 0.0 us)
Async XLA Ops:
  6.5 5.0 copy-start.1
  6.5 304.7 %all-gather.2.cloned.1.call-start = ((), (), s32[]{:S(2)}) async-start(), calls=%async_computation.1 | async-start | bytes 23592960 | tf_op jit(solution)/shard_map/all_gather | solution.py:108
  85.9 2.3 copy-start
  105.4 429.0 %all-reduce.2.cloned.1.call-start = ((), (), s32[]{:S(2)}) async-start(), calls=%async_computation.2 | async-start | bytes 16777216 | tf_op jit(solution)/shard_map/psum | solution.py:131
  236.7 102.5 %copy-start.3 = (f32[8192]{0:T(1024)S(1)}, f32[8192]{0:T(1024)}, u32[]{:S(2)}) copy-start(f32[8192]{0:T(1024)} %param.12) | copy-start | bytes 98308
  351.2 1.1 copy-start.2
Sparse Core Ops, SparseCore 0:
  105.5 205.7 all-gather.1
  371.2 163.0 all-reduce.1
where the time goes:
time: 553 us; the launch traced here: 549 us
  waiting for transfers between devices  238 us (43%)
  local copies, waits for them, and re-layouts  135 us (24%)
  blocking collectives  90 us (16%)
  other arithmetic  45.5 us (8%)
  matrix products  26 us (5%)
  between operations  14.2 us (3%)
    psum x1, waiting for transfers between devices, local(): total = lax.psum(partial_value.astype(jnp.bfloat16), 'tensor')  163 us
    all_gather x1, waiting for transfers between devices, local(): lax.all_gather(levels, 'dp', axis=0, tiled=True)  74.6 us
    all_to_all x1, blocking collectives, local(): lax.all_to_all(outgoing, 'tensor', split_axis=1, concat_axis=0, tiled=True)  69.2 us
    unnamed x15, local copies, waits for them, and re-layouts  65.2 us
    mul x2, local copies, waits for them, and re-layouts, dequantize(): shaped * scales.astype(jnp.float32)[:, None, :, None]  56.8 us
    convert_element_type x1, other arithmetic, dequantize(): return (shaped * scales.astype(jnp.float32)[:, None, :, None]).astype(jnp...  27.9 us
    all_gather x1, blocking collectives, local(): lax.all_gather(scales, 'dp', axis=0, tiled=True)  20.7 us
    dot_general x1, matrix products, local(): jnp.dot(normed, own_rows[:, :proj_cols], preferred_element_type=jnp.float32)  12 us
  transfers between devices with their start and end apart: 2, of which 2 were waited for; matrix products, arithmetic and copies ran while one was open for 20% of the time, Pallas kernels for 0%

commit v1 on v0

v1 whole, which is shorter than its diff:
```python
import functools

import jax
import jax.numpy as jnp
from jax import lax
from jax.experimental import pallas as pl
from jax.experimental.pallas import tpu as pltpu
from jax.sharding import PartitionSpec as P

D = 8192
HQ = 64
KV = 8
HD = 128
TILE = 128
TOK = 512
GROUPS = 16
GCOLS = 512
WCOLS = 640
ROWS = 64
THETA = 1000000.0
NORM_EPS = 1e-06
PEAK_EPS = 1e-06
LEVEL_TOP = 127.0
MESH = pl.DeviceIdType.MESH
QT = 64
KT = 8


def kernel(
    len_ref, hid_hbm, gain, wq, wk, wv, wo, bq, bk, bv, cos, sin, out,
    wf, pm, pk_own, pk_oth, sc, hid, send_a, wbuf, send_o, wobuf, acc, qb, kv_own, kv_oth, att, acc2, outb,
    ld_sem, pk_sem, a_send, a_recv, b_send, b_recv, sib_sem, o_send, o_recv, kv_sem, t_send, t_recv, g_send, g_recv, g_loc,
):
    dp = lax.axis_index("dp")
    t = lax.axis_index("tensor")
    xl, y = dp // 4, dp % 4
    xh, z, c = t // 8, (t // 2) % 4, t % 2

    def dev(xl_, y_, xh_, z_, c_):
        return (xl_ * 4 + y_, xh_ * 8 + z_ * 2 + c_)

    y_up, y_dn, y_op = (y + 1) % 4, (y + 3) % 4, (y + 2) % 4
    z_up, z_dn, z_op = (z + 1) % 4, (z + 3) % 4, (z + 2) % 4
    dev_yu, dev_yd = dev(xl, y_up, xh, z, c), dev(xl, y_dn, xh, z, c)
    dev_xp = dev(1 - xl, y, (xh + c) % 2, z, c)
    dev_zu, dev_zd = dev(xl, y, xh, z_up, c), dev(xl, y, xh, z_dn, c)
    dev_xh = dev(xl, y, 1 - xh, z, c)
    dev_sib = dev(xl, y, xh, z, 1 - c)
    dev_kv = dev(xl, y, (xh + xl) % 2, z, 1 - c)

    def group_of(t_):
        return ((t_ // 8 + (t_ % 2) * xl) % 2) * 8 + t_ % 8

    def remote(src, dst, ss, rs, device):
        return pltpu.make_async_remote_copy(
            src_ref=src, dst_ref=dst, send_sem=ss, recv_sem=rs, device_id=device, device_id_type=MESH
        )

    loads = (
        pltpu.make_async_copy(wq, wf.at[:, 0:8192], ld_sem.at[0]),
        pltpu.make_async_copy(wk, wf.at[:, 8192:9216], ld_sem.at[1]),
        pltpu.make_async_copy(wv, wf.at[:, 9216:10240], ld_sem.at[2]),
        pltpu.make_async_copy(wo, wf.at[:, 10240:18432], ld_sem.at[3]),
        pltpu.make_async_copy(hid_hbm, hid, ld_sem.at[4]),
    )
    for cp in loads:
        cp.start()

    barrier = pltpu.get_barrier_semaphore()

    @pl.loop(1, 16)
    def _(i):
        pl.semaphore_signal(barrier, inc=1, device_id=(dp, (t + i) % 16), device_id_type=MESH)

    for peer in (dev_yu, dev_yd, dev_xp):
        pl.semaphore_signal(barrier, inc=1, device_id=peer, device_id_type=MESH)

    for cp in loads[:4]:
        cp.wait()

    @pl.loop(0, 144, unroll=4)
    def _(j):
        tile = jnp.abs(wf[:, pl.ds(pl.multiple_of(j * 128, 128), 128)])
        pm[j] = jnp.max(tile.reshape(8, 8, 128), axis=0)

    peaks = jnp.max(jnp.max(pm[...], axis=1), axis=1, keepdims=True)
    pk_own[...] = jnp.broadcast_to(peaks, (144, 128))

    pl.semaphore_wait(barrier, 18)
    swap = remote(pk_own, pk_oth, pk_sem.at[0], pk_sem.at[1], dev_sib)
    swap.start()
    swap.wait()
    full = jnp.maximum(pk_own[...], pk_oth[...])
    sc[...] = ((full + PEAK_EPS) / LEVEL_TOP).astype(jnp.bfloat16).astype(jnp.float32)

    def quantized(j):
        tile = wf[:, pl.ds(pl.multiple_of(j * 128, 128), 128)]
        s = sc[pl.ds(j, 1), :]
        return (jnp.floor(tile / s + 0.5) * s).astype(jnp.bfloat16)

    my_rows = pl.ds(pl.multiple_of(dp * 1024 + t * 64, 64), 64)

    @pl.loop(0, 16)
    def _(i):
        to = (t + i) % 16
        g = group_of(to)
        for n in range(4):
            send_a[g, :, n * 128 : (n + 1) * 128] = quantized(g * 4 + n)
        send_a[g, :, 512:640] = quantized(QT + KT * (to % 2) + g // 2)

        @pl.when(i == 0)
        def _():
            pltpu.make_async_copy(send_a.at[g], wbuf.at[my_rows], a_recv.at[t]).start()

        @pl.when(i > 0)
        def _():
            remote(send_a.at[g], wbuf.at[my_rows], a_send.at[to], a_recv.at[t], (dp, to)).start()

    source = y % 2 == c
    slot = y // 2

    @pl.loop(0, 64)
    def _(j):
        send_o[:, pl.ds(pl.multiple_of(j * 128, 128), 128)] = quantized(QT + 2 * KT + j)

    half_rows = pl.ds(pl.multiple_of((y // 2) * 128 + c * 64, 64), 64)

    @pl.when(source)
    def _():
        pltpu.make_async_copy(send_o, wobuf.at[half_rows], sib_sem.at[0]).start()

    @pl.when(jnp.logical_not(source))
    def _():
        remote(send_o, wobuf.at[half_rows], sib_sem.at[1], sib_sem.at[2], dev_sib).start()

    loads[4].wait()

    @pl.loop(0, 32)
    def _(i):
        rows = pl.ds(pl.multiple_of(i * 16, 16), 16)
        wide = hid[rows, :].astype(jnp.float32)
        ms = jnp.mean(wide * wide, axis=1, keepdims=True)
        hid[rows, :] = (wide * lax.rsqrt(ms + NORM_EPS) * gain[...]).astype(jnp.bfloat16)

    def b_rows(xl_, y_, k):
        return pl.ds(pl.multiple_of((xl_ * 4 + y_) * 1024 + k * 256, 256), 256)

    def b_copy(y_, k, n, side, device):
        ref = wbuf.at[b_rows(xl, y_, k)]
        return remote(ref, ref, b_send.at[n], b_recv.at[side, y_, k], device)

    def b_wait(side, y_, k):
        xs = xl if side == 0 else 1 - xl
        ref = wbuf.at[b_rows(xs, y_, k)]
        remote(ref, ref, b_send.at[0], b_recv.at[side, y_, k], dev_xp).wait_recv()

    def project(xl_, y_, first=False):
        base = (xl_ * 4 + y_) * 1024
        for n in range(2):
            cols = pl.ds(pl.multiple_of(base + n * 512, 512), 512)
            part = jnp.dot(hid[:, cols], wbuf[cols, :], preferred_element_type=jnp.float32)
            if first and n == 0:
                acc[...] = part
            else:
                acc[...] += part

    @pl.loop(0, 4)
    def _(k):
        @pl.loop(0, 4)
        def _(n):
            src_t = k * 4 + n
            rows = pl.ds(pl.multiple_of(dp * 1024 + src_t * 64, 64), 64)
            ref = wbuf.at[rows]
            remote(ref, ref, a_send.at[0], a_recv.at[src_t], dev_xp).wait_recv()

        b_copy(y, k, 7 * k, 0, dev_yu).start()
        b_copy(y, k, 7 * k + 1, 0, dev_yd).start()
        b_copy(y, k, 7 * k + 2, 1, dev_xp).start()

    @pl.loop(0, 4)
    def _(k):
        b_wait(0, y_dn, k)
        b_copy(y_dn, k, 7 * k + 3, 1, dev_xp).start()

        @pl.when(k < 2)
        def _():
            b_copy(y_dn, k, 7 * k + 4, 0, dev_yu).start()

        b_wait(0, y_up, k)
        b_copy(y_up, k, 7 * k + 5, 1, dev_xp).start()

        @pl.when(k >= 2)
        def _():
            b_copy(y_up, k, 7 * k + 4, 0, dev_yd).start()

    project(xl, y, first=True)

    @pl.loop(0, 4)
    def _(k):
        b_wait(0, y_op, k)
        b_copy(y_op, k, 7 * k + 6, 1, dev_xp).start()

    def o_rows(side, s, k):
        return pl.ds(pl.multiple_of(side * 256 + s * 128 + k * 32, 32), 32)

    def o_copy(s, k, n, side, device):
        return remote(
            wobuf.at[o_rows(0, s, k)], wobuf.at[o_rows(side, s, k)], o_send.at[n], o_recv.at[side, s, k], device
        )

    def o_wait(side, s, k):
        ref = wobuf.at[o_rows(side, s, k)]
        remote(ref, ref, o_send.at[0], o_recv.at[side, s, k], dev_xp).wait_recv()

    @pl.when(source)
    def _():
        pltpu.make_async_copy(send_o, wobuf.at[half_rows], sib_sem.at[0]).wait()
        remote(send_o, wobuf.at[half_rows], sib_sem.at[1], sib_sem.at[2], dev_sib).wait_recv()

        @pl.loop(0, 4)
        def _(k):
            o_copy(slot, k, 4 * k, 0, dev_yu).start()
            o_copy(slot, k, 4 * k + 1, 0, dev_yd).start()
            o_copy(slot, k, 4 * k + 2, 1, dev_xp).start()

    @pl.loop(1, 4)
    def _(n):
        project(xl, (y + n) % 4)

    @pl.loop(0, 4)
    def _(n):
        src_y = (y + jnp.where(n == 1, 3, jnp.where(n == 2, 1, jnp.where(n == 3, 2, 0)))) % 4

        @pl.loop(0, 4)
        def _(k):
            b_wait(1, src_y, k)

        project(1 - xl, src_y)

    g_me = group_of(t)

    def rotated(x):
        return x * cos[...] + pltpu.roll(x, 64, 1) * sin[...]

    bias_kv = jnp.where(c == 0, bk[pl.ds(g_me // 2, 1), :], bv[pl.ds(g_me // 2, 1), :])
    raw = acc[:, 512:640] + bias_kv
    kv_own[...] = jnp.where(c == 0, rotated(raw), raw).astype(jnp.bfloat16)
    kv_swap = remote(kv_own, kv_oth, kv_sem.at[0], kv_sem.at[1], dev_kv)
    kv_swap.start()

    for h in range(4):
        cols = slice(h * 128, (h + 1) * 128)
        raw_q = acc[:, cols] + bq[pl.ds(g_me * 4 + h, 1), :]
        qb[:, cols] = rotated(raw_q).astype(jnp.bfloat16)

    @pl.when(jnp.logical_not(source))
    def _():
        s_dn, s_up = y_dn // 2, y_up // 2

        @pl.loop(0, 4)
        def _(k):
            o_wait(0, s_dn, k)
            o_copy(s_dn, k, 4 * k, 1, dev_xp).start()

            @pl.when(k < 2)
            def _():
                o_copy(s_dn, k, 4 * k + 1, 0, dev_yu).start()

            o_wait(0, s_up, k)
            o_copy(s_up, k, 4 * k + 2, 1, dev_xp).start()

            @pl.when(k >= 2)
            def _():
                o_copy(s_up, k, 4 * k + 1, 0, dev_yd).start()

    kv_swap.wait()
    keys = jnp.where(c == 0, kv_own[...], kv_oth[...])
    values = jnp.where(c == 0, kv_oth[...], kv_own[...])
    kv_own[...] = keys
    kv_oth[...] = values

    length = len_ref[0]

    @pl.loop(0, 4)
    def _(h):
        cols = pl.ds(pl.multiple_of(h * 128, 128), 128)
        for n in range(2):
            lo, hi = n * 256, (n + 1) * 256
            s = lax.dot_general(
                qb[lo:hi, cols], kv_own[0:hi, :], (((1,), (1,)), ((), ())), preferred_element_type=jnp.float32
            ) * HD ** (-0.5)
            r = lax.broadcasted_iota(jnp.int32, (256, hi), 0) + lo
            k = lax.broadcasted_iota(jnp.int32, (256, hi), 1)
            s = jnp.where((k <= r) & (k < length), s, -1e30)
            e = jnp.exp(s - jnp.max(s, axis=1, keepdims=True))
            p = (e / jnp.sum(e, axis=1, keepdims=True)).astype(jnp.bfloat16)
            o = jnp.dot(p, kv_oth[0:hi, :], preferred_element_type=jnp.float32)
            att[g_me, lo:hi, cols] = o.astype(jnp.bfloat16)

    def t_ref(src_t, h):
        return att.at[group_of(src_t), pl.ds(pl.multiple_of(h * 256, 256), 256)]

    def t_copy(src_t, h, n, device):
        ref = t_ref(src_t, h)
        return remote(ref, ref, t_send.at[n], t_recv.at[src_t, h], device)

    def t_wait(src_t, h):
        ref = t_ref(src_t, h)
        remote(ref, ref, t_send.at[0], t_recv.at[src_t, h], dev_sib).wait_recv()

    def tid(xh_, z_, c_):
        return xh_ * 8 + z_ * 2 + c_

    def plane_gather(copy, wait, chunks, own_started):
        low = chunks // 2
        if not own_started:

            @pl.loop(0, chunks)
            def _(h):
                start_own(copy, h)

        for s in range(2):
            xs = xh if s == 0 else 1 - xh
            if s == 1:

                @pl.loop(0, chunks)
                def _(h):
                    src = tid(xs, z, c)
                    wait(src, h)
                    copy(src, h, 15 * h + 4, dev_zu).start()
                    copy(src, h, 15 * h + 5, dev_zd).start()
                    copy(src, h, 15 * h + 6, dev_sib).start()

            @pl.loop(0, chunks)
            def _(h):
                dn, up = tid(xs, z_dn, c), tid(xs, z_up, c)
                wait(dn, h)

                @pl.when(h < low)
                def _():
                    copy(dn, h, 15 * h + 7 + 4 * s, dev_zu).start()

                copy(dn, h, 15 * h + 8 + 4 * s, dev_sib).start()
                wait(up, h)

                @pl.when(h >= low)
                def _():
                    copy(up, h, 15 * h + 7 + 4 * s, dev_zd).start()

                copy(up, h, 15 * h + 9 + 4 * s, dev_sib).start()

        for s in range(2):
            xs = xh if s == 0 else 1 - xh

            @pl.loop(0, chunks)
            def _(h):
                op = tid(xs, z_op, c)
                wait(op, h)
                copy(op, h, 15 * h + 10 + 4 * s, dev_sib).start()

    def start_own(copy, h):
        copy(t, h, 15 * h, dev_xh).start()
        copy(t, h, 15 * h + 1, dev_zu).start()
        copy(t, h, 15 * h + 2, dev_zd).start()
        copy(t, h, 15 * h + 3, dev_sib).start()

    def wait_sibling(wait, chunks):
        @pl.loop(0, 8)
        def _(n):
            @pl.loop(0, chunks)
            def _(h):
                wait(n * 2 + 1 - c, h)

    @pl.loop(0, 2)
    def _(h):
        start_own(t_copy, h)

    @pl.when(source)
    def _():
        @pl.loop(0, 4)
        def _(k):
            o_wait(0, 1 - slot, k)
            o_copy(1 - slot, k, 4 * k + 3, 1, dev_xp).start()

    plane_gather(t_copy, t_wait, 2, True)
    wait_sibling(t_wait, 2)

    @pl.loop(0, 4)
    def _(k):
        o_wait(1, 0, k)
        o_wait(1, 1, k)

    def out_block(src_t, j):
        xh_s, z_s, c_s = src_t // 8, (src_t // 2) % 4, src_t % 2
        side, s = j // 2, j % 2
        xl_b = (xl + side) % 2
        xh_b = (xh_s + side * c_s) % 2
        return (xl_b * 4 + c_s + 2 * s) * 8 + xh_b * 4 + z_s

    def g_ref(src_t, j):
        return out.at[:, pl.ds(pl.multiple_of(out_block(src_t, j) * 128, 128), 128)]

    def g_copy_own(src_t, j, n, device):
        return remote(outb.at[j], g_ref(src_t, j), g_send.at[n], g_recv.at[src_t, j], device)

    def g_copy(src_t, j, n, device):
        ref = g_ref(src_t, j)
        return remote(ref, ref, g_send.at[n], g_recv.at[src_t, j], device)

    def g_wait(src_t, j):
        ref = g_ref(src_t, j)
        remote(ref, ref, g_send.at[0], g_recv.at[src_t, j], dev_sib).wait_recv()

    for half in range(2):

        @pl.loop(0, 16)
        def _(g):
            part = lax.dot_general(
                att[g],
                wobuf[half * 256 : (half + 1) * 256, pl.ds(pl.multiple_of(g * 512, 512), 512)],
                (((1,), (1,)), ((), ())),
                preferred_element_type=jnp.float32,
            )
            acc2[...] = jnp.where(g == 0, part, acc2[...] + part)

        for n in range(2):
            j = half * 2 + n
            outb[j] = acc2[:, n * 128 : (n + 1) * 128].astype(jnp.bfloat16)
            pltpu.make_async_copy(outb.at[j], g_ref(t, j), g_loc.at[j]).start()
            start_own(g_copy_own, j)

    plane_gather(g_copy, g_wait, 4, True)
    wait_sibling(g_wait, 4)

    for j in range(4):
        pltpu.make_async_copy(outb.at[j], g_ref(t, j), g_loc.at[j]).wait()

    def drain(ref, sem):
        remote(ref, ref, sem, sem, dev_sib).wait_send()

    @pl.loop(1, 16)
    def _(i):
        drain(send_a.at[0], a_send.at[(t + i) % 16])

    @pl.when(jnp.logical_not(source))
    def _():
        drain(send_o, sib_sem.at[1])

    @pl.loop(0, 28)
    def _(n):
        drain(wbuf.at[0:256], b_send.at[n])

    @pl.loop(0, 4)
    def _(k):
        for n in range(3):
            drain(wobuf.at[0:32], o_send.at[4 * k + n])

        @pl.when(source)
        def _():
            drain(wobuf.at[0:32], o_send.at[4 * k + 3])

    @pl.loop(0, 30)
    def _(n):
        drain(att.at[0, 0:256], t_send.at[n])

    @pl.loop(0, 60)
    def _(n):
        drain(outb.at[0], g_send.at[n])


def local(hidden, lengths, norm_gain, w_q, w_k, w_v, w_out, b_q, b_k, b_v):
    positions = jnp.arange(TOK).astype(jnp.float32)
    freqs = THETA ** (-jnp.arange(0, HD, 2).astype(jnp.float32) / HD)
    angles = positions[:, None] * freqs[None, :]
    cosine, sine = jnp.cos(angles), jnp.sin(angles)
    cos = jnp.concatenate((cosine, cosine), axis=1)
    sin = jnp.concatenate((-sine, sine), axis=1)
    anywhere = pl.BlockSpec(memory_space=pl.ANY)
    vmem = pl.BlockSpec(memory_space=pltpu.VMEM)
    bf, f32 = jnp.bfloat16, jnp.float32
    dma = pltpu.SemaphoreType.DMA
    result = pl.pallas_call(
        kernel,
        out_shape=jax.ShapeDtypeStruct((TOK, D), bf),
        in_specs=[pl.BlockSpec(memory_space=pltpu.SMEM), anywhere, vmem]
        + [anywhere] * 4
        + [vmem] * 5,
        out_specs=anywhere,
        scratch_shapes=[
            pltpu.VMEM((ROWS, 18432), f32),
            pltpu.VMEM((144, 8, 128), f32),
            pltpu.VMEM((144, 128), f32),
            pltpu.VMEM((144, 128), f32),
            pltpu.VMEM((144, 128), f32),
            pltpu.VMEM((TOK, D), bf),
            pltpu.VMEM((GROUPS, ROWS, WCOLS), bf),
            pltpu.VMEM((D, WCOLS), bf),
            pltpu.VMEM((ROWS, D), bf),
            pltpu.VMEM((512, D), bf),
            pltpu.VMEM((TOK, WCOLS), f32),
            pltpu.VMEM((TOK, GCOLS), bf),
            pltpu.VMEM((TOK, HD), bf),
            pltpu.VMEM((TOK, HD), bf),
            pltpu.VMEM((GROUPS, TOK, GCOLS), bf),
            pltpu.VMEM((TOK, 256), f32),
            pltpu.VMEM((4, TOK, 128), bf),
            dma((5,)),
            dma((2,)),
            dma((16,)),
            dma((16,)),
            dma((28,)),
            dma((2, 4, 4)),
            dma((3,)),
            dma((16,)),
            dma((2, 2, 4)),
            dma((2,)),
            dma((30,)),
            dma((16, 2)),
            dma((60,)),
            dma((16, 4)),
            dma((4,)),
        ],
        compiler_params=pltpu.CompilerParams(
            collective_id=0, has_side_effects=True, vmem_limit_bytes=62 * 2**20
        ),
    )(
        lengths, hidden[0], norm_gain.reshape(1, D), w_q, w_k, w_v, w_out,
        b_q.reshape(HQ, HD), b_k.reshape(KV, HD), b_v.reshape(KV, HD), cos, sin,
    )
    return result[None]


def solution(mesh):
    rows = P(("dp", "tensor"), None)
    placed = (P("dp", None, None), P("dp"), P(), rows, rows, rows, rows, P(), P(), P())
    return jax.shard_map(
        local, mesh=mesh, in_specs=placed, out_specs=P("dp", None, None), check_vma=False
    )
```

time: 553 us -> 220 us (0.40)
  waiting for transfers between devices: 238 us -> 0 us
  Pallas kernels: 0 us -> 209 us
  local copies, waits for them, and re-layouts: 135 us -> 7.77 us
  blocking collectives: 90 us -> 0 us
  other arithmetic: 45.5 us -> 2.02 us
  matrix products: 26 us -> 0 us
  between operations: 14.2 us -> 0.68 us
    pallas_call x0 -> x1, Pallas kernels: none -> 209 us  [local(): pl.pallas_call(kernel, out_shape=jax.ShapeDtypeStruct((TOK, D), bf), in_s...]
    psum x1 -> x0, waiting for transfers between devices: 163 us -> none  [local(): total = lax.psum(partial_value.astype(jnp.bfloat16), 'tensor')]
    all_gather x1 -> x0, waiting for transfers between devices: 74.6 us -> none  [local(): lax.all_gather(levels, 'dp', axis=0, tiled=True)]
    all_to_all x1 -> x0, blocking collectives: 69.2 us -> none  [local(): lax.all_to_all(outgoing, 'tensor', split_axis=1, concat_axis=0, tiled=True)]
    unnamed x15 -> x1, local copies, waits for them, and re-layouts: 65.2 us -> 7.77 us
    mul x2 -> x0, local copies, waits for them, and re-layouts: 56.8 us -> none  [dequantize(): shaped * scales.astype(jnp.float32)[:, None, :, None]]
    convert_element_type x4 -> x1, other arithmetic: 34.4 us -> 0.01 us  [local(): positions = jnp.arange(TOK).astype(jnp.float32)]
    dot_general x4 -> x0, matrix products: 26 us -> none  [the longest x1 12 us: local(): jnp.dot(normed, own_rows[:, :proj_cols], preferred_element_type=jnp.float32)]
  transfers between devices with their start and end apart: 2 -> 0, of which waited for: 2 -> 0; matrix products, arithmetic and copies ran while one was open for 20% -> 0% of each run, Pallas kernels for 0% -> 0%
where the time goes in v1:
time: 220 us
  Pallas kernels  209 us (95%)
  local copies, waits for them, and re-layouts  7.77 us (4%)
    pallas_call x1, Pallas kernels, local(): pl.pallas_call(kernel, out_shape=jax.ShapeDtypeStruct((TOK, D), bf), in_s...  209 us
    unnamed x1, local copies, waits for them, and re-layouts  7.77 us

profile of v1, /device:TPU:27, one launch (start us, length us, event | category | flops | bytes accessed | tf_op | source)
XLA Modules:
  0.0 219.6 jit_solution(3170136937802340848)
XLA Ops:
  0.7 1.0 fusion
  1.7 1.0 pad_maximum_fusion
  2.7 209.1 %shard_map.100 = bf16[512,8192]{1,0:T(8,128)(2,1)} custom-call(s32[1]{0:T(128)S(6)} %copy.12.len_ref, bf16[512,8192]{1,0:T(8,128)(2,1)} %bitcast.7, f32[1,8192]{1,0:T(1,128)} %bitcast.8, f32[64,8192]{1,0:T(8,128)} %wq.1, f32[64,1024]{1,0:T(8,128)} %wk.1, f32[64,1024]{1,0:T(8,128)} %wv.1, f32[64,8192]{1,0:T(8,128)} %wo.1, f32[64,128]{1,0:T(8,128)} %bitcast.9, ...), custom_call_target="tpu_custom_call" | custom-call | tf_op jit(solution)/shard_map/pallas_call | solution.py:482
  211.8 7.8 %copy.13 = bf16[1,512,8192]{2,1,0:T(8,128)(2,1)} copy(bf16[1,512,8192]{2,1,0:T(8,128)(2,1)} %bitcast.6) | data formatting | bytes 16777216
  (2 shorter events, 0.0 us)

commit v2 on v1

v2 whole, which is shorter than its diff:
```python
import functools

import jax
import jax.numpy as jnp
import numpy as np
from jax import lax
from jax.experimental import pallas as pl
from jax.experimental.pallas import tpu as pltpu
from jax.sharding import PartitionSpec as P

D = 8192
HQ = 64
KV = 8
HD = 128
TILE = 128
TOK = 512
GROUPS = 16
GCOLS = 512
WCOLS = 640
ROWS = 64
THETA = 1000000.0
NORM_EPS = 1e-06
PEAK_EPS = 1e-06
LEVEL_TOP = 127.0
MESH = pl.DeviceIdType.MESH
QT = 64
KT = 8
Q_CHUNKS = 8
Q_FIRST = 3
O_CHUNKS = 4
O_FIRST = 2
G_FIRST = 2


def kernel(
    len_ref, hid_hbm, gain, wq, wk, wv, wo, bq, bk, bv, cos, sin, out,
    wf, pm, pk_own, pk_oth, sc, hid, send_a, wbuf, send_o, wobuf, acc, qb, kv_own, kv_oth, att, acc2, outb,
    ld_sem, pk_sem, a_send, a_recv, b_send, b_recv, sib_sem, o_send, o_recv, kv_sem, t_send, t_recv, g_send, g_recv, g_loc,
):
    dp = lax.axis_index("dp")
    t = lax.axis_index("tensor")
    xl, y = dp // 4, dp % 4
    xh, z, c = t // 8, (t // 2) % 4, t % 2

    def dev(xl_, y_, xh_, z_, c_):
        return (xl_ * 4 + y_, xh_ * 8 + z_ * 2 + c_)

    y_up, y_dn, y_op = (y + 1) % 4, (y + 3) % 4, (y + 2) % 4
    z_up, z_dn, z_op = (z + 1) % 4, (z + 3) % 4, (z + 2) % 4
    dev_yu, dev_yd = dev(xl, y_up, xh, z, c), dev(xl, y_dn, xh, z, c)
    dev_xp = dev(1 - xl, y, (xh + c) % 2, z, c)
    dev_zu, dev_zd = dev(xl, y, xh, z_up, c), dev(xl, y, xh, z_dn, c)
    dev_xh = dev(xl, y, 1 - xh, z, c)
    dev_sib = dev(xl, y, xh, z, 1 - c)
    dev_kv = dev(xl, y, (xh + xl) % 2, z, 1 - c)

    def group_of(t_):
        return ((t_ // 8 + (t_ % 2) * xl) % 2) * 8 + t_ % 8

    def remote(src, dst, ss, rs, device):
        return pltpu.make_async_remote_copy(
            src_ref=src, dst_ref=dst, send_sem=ss, recv_sem=rs, device_id=device, device_id_type=MESH
        )

    loads = (
        pltpu.make_async_copy(wq, wf.at[:, 0:8192], ld_sem.at[0]),
        pltpu.make_async_copy(wk, wf.at[:, 8192:9216], ld_sem.at[1]),
        pltpu.make_async_copy(wv, wf.at[:, 9216:10240], ld_sem.at[2]),
        pltpu.make_async_copy(wo, wf.at[:, 10240:18432], ld_sem.at[3]),
        pltpu.make_async_copy(hid_hbm, hid, ld_sem.at[4]),
    )
    for cp in loads:
        cp.start()

    barrier = pltpu.get_barrier_semaphore()

    @pl.loop(1, 16)
    def _(i):
        pl.semaphore_signal(barrier, inc=1, device_id=(dp, (t + i) % 16), device_id_type=MESH)

    for peer in (dev_yu, dev_yd, dev_xp):
        pl.semaphore_signal(barrier, inc=1, device_id=peer, device_id_type=MESH)

    for cp in loads[:4]:
        cp.wait()

    @pl.loop(0, 144, unroll=4)
    def _(j):
        tile = jnp.abs(wf[:, pl.ds(pl.multiple_of(j * 128, 128), 128)])
        pm[j] = jnp.max(tile.reshape(8, 8, 128), axis=0)

    peaks = jnp.max(jnp.max(pm[...], axis=1), axis=1, keepdims=True)
    pk_own[...] = jnp.broadcast_to(peaks, (144, 128))

    pl.semaphore_wait(barrier, 18)
    swap = remote(pk_own, pk_oth, pk_sem.at[0], pk_sem.at[1], dev_sib)
    swap.start()
    swap.wait()
    full = jnp.maximum(pk_own[...], pk_oth[...])
    sc[...] = ((full + PEAK_EPS) / LEVEL_TOP).astype(jnp.bfloat16).astype(jnp.float32)

    def quantized(j):
        tile = wf[:, pl.ds(pl.multiple_of(j * 128, 128), 128)]
        s = sc[pl.ds(j, 1), :]
        return (jnp.floor(tile / s + 0.5) * s).astype(jnp.bfloat16)

    my_rows = pl.ds(pl.multiple_of(dp * 1024 + t * 64, 64), 64)

    hx = (xh + c * xl) % 2

    def ring(step):
        return jnp.where(step == 1, 3, jnp.where(step == 2, 1, jnp.where(step == 3, 2, 0)))

    @pl.loop(0, 16)
    def _(i):
        to_c = i % 2
        to = ((xh + i // 8 + to_c * xl) % 2) * 8 + ((z + 4 - ring((i // 2) % 4)) % 4) * 2 + to_c
        g = group_of(to)
        for n in range(4):
            send_a[g, :, n * 128 : (n + 1) * 128] = quantized(g * 4 + n)
        send_a[g, :, 512:640] = quantized(QT + KT * to_c + g // 2)

        @pl.when(to == t)
        def _():
            pltpu.make_async_copy(send_a.at[g], wbuf.at[my_rows], a_recv.at[t]).start()

        @pl.when(to != t)
        def _():
            remote(send_a.at[g], wbuf.at[my_rows], a_send.at[to], a_recv.at[t], (dp, to)).start()

    source = y % 2 == c
    slot = y // 2

    @pl.loop(0, 64)
    def _(j):
        send_o[:, pl.ds(pl.multiple_of(j * 128, 128), 128)] = quantized(QT + 2 * KT + j)

    half_rows = pl.ds(pl.multiple_of((y // 2) * 128 + c * 64, 64), 64)

    @pl.when(source)
    def _():
        pltpu.make_async_copy(send_o, wobuf.at[half_rows], sib_sem.at[0]).start()

    @pl.when(jnp.logical_not(source))
    def _():
        remote(send_o, wobuf.at[half_rows], sib_sem.at[1], sib_sem.at[2], dev_sib).start()

    loads[4].wait()

    @pl.loop(0, 32)
    def _(i):
        rows = pl.ds(pl.multiple_of(i * 16, 16), 16)
        wide = hid[rows, :].astype(jnp.float32)
        ms = jnp.mean(wide * wide, axis=1, keepdims=True)
        hid[rows, :] = (wide * lax.rsqrt(ms + NORM_EPS) * gain[...]).astype(jnp.bfloat16)

    def o_rows(side, s, k):
        return pl.ds(pl.multiple_of(side * 256 + s * 128 + k * 32, 32), 32)

    def o_copy(side, s, k, n, device, to_side):
        return remote(
            wobuf.at[o_rows(side, s, k)], wobuf.at[o_rows(to_side, s, k)], o_send.at[n],
            o_recv.at[to_side, s, k], device,
        )

    def o_wait(side, s, k):
        ref = wobuf.at[o_rows(side, s, k)]
        remote(ref, ref, o_send.at[0], o_recv.at[side, s, k], dev_xp).wait_recv()

    s_dn, s_up = y_dn // 2, y_up // 2

    def o_forward(side, k, n):
        @pl.when(k % 2 == 0)
        def _():
            o_copy(side, s_dn, k, n, dev_yu, side).start()

        @pl.when(k % 2 == 1)
        def _():
            o_copy(side, s_up, k, n, dev_yd, side).start()

    def b_chip(j):
        return ((hx + j // 4) % 2) * 4 + (z + ring(j % 4)) % 4

    def b_rows(side, y_, j):
        return pl.ds(pl.multiple_of((((xl + side) % 2) * 4 + y_) * 1024 + b_chip(j) * 128, 128), 128)

    def b_copy(side, y_, j, n, device, to_side):
        ref = wbuf.at[b_rows(side, y_, j)]
        return remote(ref, ref, b_send.at[n], b_recv.at[to_side, y_, j], device)

    def b_wait(side, y_, j):
        ref = wbuf.at[b_rows(side, y_, j)]
        remote(ref, ref, b_send.at[0], b_recv.at[side, y_, j], dev_xp).wait_recv()

    def b_forward(side, j, n):
        @pl.when(j % 2 == 0)
        def _():
            b_copy(side, y_dn, j, n, dev_yu, side).start()

        @pl.when(j % 2 == 1)
        def _():
            b_copy(side, y_up, j, n, dev_yd, side).start()

    def project(side, y_, first=False):
        base = (((xl + side) % 2) * 4 + y_) * 1024
        for n in range(2):
            cols = pl.ds(pl.multiple_of(base + n * 512, 512), 512)
            part = jnp.dot(hid[:, cols], wbuf[cols, :], preferred_element_type=jnp.float32)
            if first and n == 0:
                acc[...] = part
            else:
                acc[...] += part

    @pl.loop(0, Q_CHUNKS)
    def _(j):
        @pl.loop(0, 2)
        def _(n):
            src_t = b_chip(j) * 2 + n
            rows = pl.ds(pl.multiple_of(dp * 1024 + src_t * 64, 64), 64)
            ref = wbuf.at[rows]
            remote(ref, ref, a_send.at[0], a_recv.at[src_t], dev_xp).wait_recv()

        b_copy(0, y, j, 3 * j, dev_xp, 1).start()
        b_copy(0, y, j, 3 * j + 1, dev_yu, 0).start()
        b_copy(0, y, j, 3 * j + 2, dev_yd, 0).start()

    @pl.when(source)
    def _():
        pltpu.make_async_copy(send_o, wobuf.at[half_rows], sib_sem.at[0]).wait()
        remote(send_o, wobuf.at[half_rows], sib_sem.at[1], sib_sem.at[2], dev_sib).wait_recv()

        @pl.loop(0, O_FIRST)
        def _(k):
            o_copy(0, slot, k, 4 * k + 2, dev_xp, 1).start()

    @pl.loop(0, Q_FIRST)
    def _(j):
        n = 24 + 4 * j
        b_wait(1, y, j)
        b_copy(1, y, j, n, dev_yu, 1).start()
        b_copy(1, y, j, n + 1, dev_yd, 1).start()
        b_wait(0, y_dn, j)
        b_wait(0, y_up, j)
        b_forward(0, j, n + 2)

    @pl.loop(Q_FIRST, Q_CHUNKS)
    def _(j):
        n = 24 + 4 * j
        b_wait(0, y_dn, j)
        b_copy(0, y_dn, j, n, dev_xp, 1).start()
        b_wait(0, y_up, j)
        b_copy(0, y_up, j, n + 1, dev_xp, 1).start()
        b_forward(0, j, n + 2)

    @pl.loop(0, Q_FIRST)
    def _(j):
        b_wait(1, y_dn, j)
        b_wait(1, y_up, j)
        b_forward(1, j, 24 + 4 * j + 3)

    project(0, y, first=True)

    @pl.loop(Q_FIRST, Q_CHUNKS)
    def _(j):
        b_wait(0, y_op, j)
        b_copy(0, y_op, j, 24 + 4 * j + 3, dev_xp, 1).start()

    @pl.when(source)
    def _():
        @pl.loop(0, O_CHUNKS)
        def _(k):
            o_copy(0, slot, k, 4 * k, dev_yu, 0).start()
            o_copy(0, slot, k, 4 * k + 1, dev_yd, 0).start()

        @pl.loop(0, O_FIRST)
        def _(k):
            o_wait(1, slot, k)
            o_copy(1, slot, k, 16 + 2 * k, dev_yu, 1).start()
            o_copy(1, slot, k, 17 + 2 * k, dev_yd, 1).start()

    project(0, y_dn)
    project(0, y_up)

    @pl.loop(0, Q_FIRST)
    def _(j):
        b_wait(0, y_op, j)

    project(0, y_op)

    @pl.loop(Q_FIRST, Q_CHUNKS)
    def _(j):
        b_wait(1, y, j)

    project(1, y)

    @pl.loop(0, 2)
    def _(n):
        y_ = jnp.where(n == 0, y_dn, y_up)

        @pl.loop(Q_FIRST, Q_CHUNKS)
        def _(j):
            b_wait(1, y_, j)

        project(1, y_)

    @pl.loop(0, Q_CHUNKS)
    def _(j):
        b_wait(1, y_op, j)

    project(1, y_op)

    g_me = group_of(t)

    def rotated(x):
        return x * cos[...] + pltpu.roll(x, 64, 1) * sin[...]

    bias_kv = jnp.where(c == 0, bk[pl.ds(g_me // 2, 1), :], bv[pl.ds(g_me // 2, 1), :])
    raw = acc[:, 512:640] + bias_kv
    kv_own[...] = jnp.where(c == 0, rotated(raw), raw).astype(jnp.bfloat16)
    kv_swap = remote(kv_own, kv_oth, kv_sem.at[0], kv_sem.at[1], dev_kv)
    kv_swap.start()

    for h in range(4):
        cols = slice(h * 128, (h + 1) * 128)
        raw_q = acc[:, cols] + bq[pl.ds(g_me * 4 + h, 1), :]
        qb[:, cols] = rotated(raw_q).astype(jnp.bfloat16)

    kv_swap.wait()
    keys = jnp.where(c == 0, kv_own[...], kv_oth[...])
    values = jnp.where(c == 0, kv_oth[...], kv_own[...])
    kv_own[...] = keys
    kv_oth[...] = values

    def t_ref(src_t, h):
        return att.at[group_of(src_t), pl.ds(pl.multiple_of(h * 256, 256), 256)]

    def t_copy(src_t, h, n, device):
        ref = t_ref(src_t, h)
        return remote(ref, ref, t_send.at[n], t_recv.at[src_t, h], device)

    def t_wait(src_t, h):
        ref = t_ref(src_t, h)
        remote(ref, ref, t_send.at[0], t_recv.at[src_t, h], dev_sib).wait_recv()

    def tid(xh_, z_, c_):
        return xh_ * 8 + z_ * 2 + c_

    def gather_side(copy, wait, chunks, first, side):
        xs = (xh + side) % 2
        own, dn, up = tid(xs, z, c), tid(xs, z_dn, c), tid(xs, z_up, c)
        if side == 1:

            @pl.loop(0, chunks)
            def _(h):
                wait(own, h)

                @pl.when(h < first)
                def _():
                    copy(own, h, 15 * h + 8, dev_zu).start()
                    copy(own, h, 15 * h + 9, dev_zd).start()

                copy(own, h, 15 * h + 10, dev_sib).start()

        @pl.loop(0, chunks)
        def _(h):
            n = 15 * h + 4 + 7 * side
            wait(dn, h)
            wait(up, h)
            along = h < first if side == 1 else h >= 0

            @pl.when(jnp.logical_and(along, h % 2 == 0))
            def _():
                copy(dn, h, n, dev_zu).start()

            @pl.when(jnp.logical_and(along, h % 2 == 1))
            def _():
                copy(up, h, n, dev_zd).start()

            if side == 0:

                @pl.when(h >= first)
                def _():
                    copy(dn, h, 15 * h + 8, dev_xh).start()
                    copy(up, h, 15 * h + 9, dev_xh).start()

            copy(dn, h, n + 1, dev_sib).start()
            copy(up, h, n + 2, dev_sib).start()

    def gather_last(copy, wait, chunks, first, side):
        @pl.loop(0, chunks)
        def _(h):
            op = tid((xh + side) % 2, z_op, c)
            wait(op, h)
            if side == 0:

                @pl.when(h >= first)
                def _():
                    copy(op, h, 15 * h + 11, dev_xh).start()

            copy(op, h, 15 * h + 7 + 7 * side, dev_sib).start()

    def start_own(copy, h):
        copy(t, h, 15 * h, dev_xh).start()
        copy(t, h, 15 * h + 1, dev_zu).start()
        copy(t, h, 15 * h + 2, dev_zd).start()
        copy(t, h, 15 * h + 3, dev_sib).start()

    def wait_sibling(wait, chunks):
        @pl.loop(0, 8)
        def _(n):
            @pl.loop(0, chunks)
            def _(h):
                wait(n * 2 + 1 - c, h)

    length = len_ref[0]

    for n in range(2):
        lo, hi = n * 256, (n + 1) * 256

        @pl.loop(0, 4)
        def _(h):
            cols = pl.ds(pl.multiple_of(h * 128, 128), 128)
            s = lax.dot_general(
                qb[lo:hi, cols], kv_own[0:hi, :], (((1,), (1,)), ((), ())), preferred_element_type=jnp.float32
            ) * HD ** (-0.5)
            r = lax.broadcasted_iota(jnp.int32, (256, hi), 0) + lo
            k = lax.broadcasted_iota(jnp.int32, (256, hi), 1)
            s = jnp.where((k <= r) & (k < length), s, -1e30)
            e = jnp.exp(s - jnp.max(s, axis=1, keepdims=True))
            p = (e / jnp.sum(e, axis=1, keepdims=True)).astype(jnp.bfloat16)
            o = jnp.dot(p, kv_oth[0:hi, :], preferred_element_type=jnp.float32)
            att[g_me, lo:hi, cols] = o.astype(jnp.bfloat16)

        start_own(t_copy, n)

    @pl.when(source)
    def _():
        @pl.loop(O_FIRST, O_CHUNKS)
        def _(k):
            o_copy(0, slot, k, 4 * k + 2, dev_xp, 1).start()

    @pl.when(jnp.logical_not(source))
    def _():
        @pl.loop(0, O_CHUNKS)
        def _(k):
            o_wait(0, s_dn, k)
            o_wait(0, s_up, k)
            o_forward(0, k, 4 * k)

            @pl.when(k >= O_FIRST)
            def _():
                o_copy(0, s_dn, k, 4 * k + 1, dev_xp, 1).start()
                o_copy(0, s_up, k, 4 * k + 2, dev_xp, 1).start()

        @pl.loop(0, O_FIRST)
        def _(k):
            o_wait(1, s_dn, k)
            o_wait(1, s_up, k)
            o_forward(1, k, 4 * k + 1)

    gather_side(t_copy, t_wait, 2, 2, 0)

    @pl.when(source)
    def _():
        @pl.loop(0, O_CHUNKS)
        def _(k):
            o_wait(0, 1 - slot, k)

            @pl.when(k >= O_FIRST)
            def _():
                o_copy(0, 1 - slot, k, 4 * k + 3, dev_xp, 1).start()

    gather_side(t_copy, t_wait, 2, 2, 1)
    gather_last(t_copy, t_wait, 2, 2, 0)

    @pl.when(source)
    def _():
        @pl.loop(O_FIRST, O_CHUNKS)
        def _(k):
            o_wait(1, slot, k)

        @pl.loop(0, O_CHUNKS)
        def _(k):
            o_wait(1, 1 - slot, k)

    @pl.when(jnp.logical_not(source))
    def _():
        @pl.loop(O_FIRST, O_CHUNKS)
        def _(k):
            o_wait(1, s_dn, k)
            o_wait(1, s_up, k)

    def add_group(src_t, first=False):
        g = group_of(src_t)
        part = lax.dot_general(
            att[g],
            wobuf[:, pl.ds(pl.multiple_of(g * 512, 512), 512)],
            (((1,), (1,)), ((), ())),
            preferred_element_type=jnp.float32,
        )
        if first:
            acc2[...] = part
        else:
            acc2[...] += part

    def near(i):
        step = i % 4
        return (xh + i // 4) % 2, (z + ring(step)) % 4

    add_group(t, True)

    @pl.loop(1, 7)
    def _(i):
        xs, zs = near(i)
        add_group(tid(xs, zs, c))

    gather_last(t_copy, t_wait, 2, 2, 1)
    add_group(tid(1 - xh, z_op, c))

    @pl.loop(0, 8)
    def _(i):
        xs, zs = near(i)
        src = tid(xs, zs, 1 - c)
        t_wait(src, 0)
        t_wait(src, 1)
        add_group(src)

    def out_block(src_t, j):
        xh_s, z_s, c_s = src_t // 8, (src_t // 2) % 4, src_t % 2
        side, s = j // 2, j % 2
        xl_b = (xl + side) % 2
        xh_b = (xh_s + side * c_s) % 2
        return (xl_b * 4 + c_s + 2 * s) * 8 + xh_b * 4 + z_s

    def g_ref(src_t, j):
        return out.at[:, pl.ds(pl.multiple_of(out_block(src_t, j) * 128, 128), 128)]

    def g_copy_own(src_t, j, n, device):
        return remote(outb.at[j], g_ref(src_t, j), g_send.at[n], g_recv.at[src_t, j], device)

    def g_copy(src_t, j, n, device):
        ref = g_ref(src_t, j)
        return remote(ref, ref, g_send.at[n], g_recv.at[src_t, j], device)

    def g_wait(src_t, j):
        ref = g_ref(src_t, j)
        remote(ref, ref, g_send.at[0], g_recv.at[src_t, j], dev_sib).wait_recv()

    for j in range(4):
        outb[j] = acc2[:, j * 128 : (j + 1) * 128].astype(jnp.bfloat16)
        pltpu.make_async_copy(outb.at[j], g_ref(t, j), g_loc.at[j]).start()
        start_own(g_copy_own, j)

    gather_side(g_copy, g_wait, 4, G_FIRST, 0)
    gather_last(g_copy, g_wait, 4, G_FIRST, 0)
    gather_side(g_copy, g_wait, 4, G_FIRST, 1)
    gather_last(g_copy, g_wait, 4, G_FIRST, 1)
    wait_sibling(g_wait, 4)

    for j in range(4):
        pltpu.make_async_copy(outb.at[j], g_ref(t, j), g_loc.at[j]).wait()

    def drain(ref, sem):
        remote(ref, ref, sem, sem, dev_sib).wait_send()

    @pl.loop(1, 16)
    def _(i):
        drain(send_a.at[0], a_send.at[(t + i) % 16])

    @pl.when(jnp.logical_not(source))
    def _():
        drain(send_o, sib_sem.at[1])

    @pl.loop(0, 56)
    def _(n):
        drain(wbuf.at[0:128], b_send.at[n])

    @pl.when(source)
    def _():
        @pl.loop(0, O_CHUNKS)
        def _(k):
            for n in range(3):
                drain(wobuf.at[0:32], o_send.at[4 * k + n])

            @pl.when(k >= O_FIRST)
            def _():
                drain(wobuf.at[0:32], o_send.at[4 * k + 3])

            @pl.when(k < O_FIRST)
            def _():
                drain(wobuf.at[0:32], o_send.at[16 + 2 * k])
                drain(wobuf.at[0:32], o_send.at[17 + 2 * k])

    @pl.when(jnp.logical_not(source))
    def _():
        @pl.loop(0, O_CHUNKS)
        def _(k):
            drain(wobuf.at[0:32], o_send.at[4 * k])
            drain(wobuf.at[0:32], o_send.at[4 * k + 1])

            @pl.when(k >= O_FIRST)
            def _():
                drain(wobuf.at[0:32], o_send.at[4 * k + 2])

    @pl.loop(0, 30)
    def _(n):
        drain(att.at[0, 0:256], t_send.at[n])

    @pl.loop(0, 60)
    def _(n):
        drain(outb.at[0], g_send.at[n])


def local(hidden, lengths, norm_gain, w_q, w_k, w_v, w_out, b_q, b_k, b_v):
    positions = np.arange(TOK, dtype=np.float32)
    freqs = np.float32(THETA) ** (-np.arange(0, HD, 2, dtype=np.float32) / np.float32(HD))
    angles = (positions[:, None] * freqs[None, :]).astype(np.float64)
    cosine, sine = np.cos(angles), np.sin(angles)
    cos = np.concatenate((cosine, cosine), axis=1).astype(np.float32)
    sin = np.concatenate((-sine, sine), axis=1).astype(np.float32)
    anywhere = pl.BlockSpec(memory_space=pl.ANY)
    vmem = pl.BlockSpec(memory_space=pltpu.VMEM)
    bf, f32 = jnp.bfloat16, jnp.float32
    dma = pltpu.SemaphoreType.DMA
    result = pl.pallas_call(
        kernel,
        out_shape=jax.ShapeDtypeStruct((TOK, D), bf),
        in_specs=[pl.BlockSpec(memory_space=pltpu.SMEM), anywhere, vmem]
        + [anywhere] * 4
        + [vmem] * 5,
        out_specs=anywhere,
        scratch_shapes=[
            pltpu.VMEM((ROWS, 18432), f32),
            pltpu.VMEM((144, 8, 128), f32),
            pltpu.VMEM((144, 128), f32),
            pltpu.VMEM((144, 128), f32),
            pltpu.VMEM((144, 128), f32),
            pltpu.VMEM((TOK, D), bf),
            pltpu.VMEM((GROUPS, ROWS, WCOLS), bf),
            pltpu.VMEM((D, WCOLS), bf),
            pltpu.VMEM((ROWS, D), bf),
            pltpu.VMEM((512, D), bf),
            pltpu.VMEM((TOK, WCOLS), f32),
            pltpu.VMEM((TOK, GCOLS), bf),
            pltpu.VMEM((TOK, HD), bf),
            pltpu.VMEM((TOK, HD), bf),
            pltpu.VMEM((GROUPS, TOK, GCOLS), bf),
            pltpu.VMEM((TOK, GCOLS), f32),
            pltpu.VMEM((4, TOK, 128), bf),
            dma((5,)),
            dma((2,)),
            dma((16,)),
            dma((16,)),
            dma((56,)),
            dma((2, 4, Q_CHUNKS)),
            dma((3,)),
            dma((20,)),
            dma((2, 2, 4)),
            dma((2,)),
            dma((30,)),
            dma((16, 2)),
            dma((60,)),
            dma((16, 4)),
            dma((4,)),
        ],
        compiler_params=pltpu.CompilerParams(
            collective_id=0, has_side_effects=True, vmem_limit_bytes=62 * 2**20
        ),
    )(
        lengths, hidden[0], norm_gain.reshape(1, D), w_q, w_k, w_v, w_out,
        b_q.reshape(HQ, HD), b_k.reshape(KV, HD), b_v.reshape(KV, HD), cos, sin,
    )
    return result[None]


def solution(mesh):
    rows = P(("dp", "tensor"), None)
    placed = (P("dp", None, None), P("dp"), P(), rows, rows, rows, rows, P(), P(), P())
    return jax.shard_map(
        local, mesh=mesh, in_specs=placed, out_specs=P("dp", None, None), check_vma=False
    )
```

time: 220 us -> 199 us (0.905)
  Pallas kernels: 209 us -> 190 us
    pallas_call x1, Pallas kernels: 209 us -> 190 us  [local(): pl.pallas_call(kernel, out_shape=jax.ShapeDtypeStruct((TOK, D), bf), in_s...]
where the time goes in v2:
time: 199 us
  Pallas kernels  190 us (95%)
  local copies, waits for them, and re-layouts  7.77 us (4%)
    pallas_call x1, Pallas kernels, local(): pl.pallas_call(kernel, out_shape=jax.ShapeDtypeStruct((TOK, D), bf), in_s...  190 us
    unnamed x1, local copies, waits for them, and re-layouts  7.77 us

profile of v2, /device:TPU:27, one launch (start us, length us, event | category | flops | bytes accessed | tf_op | source)
XLA Modules:
  0.0 198.5 jit_solution(9991615532639663854)
XLA Ops:
  0.7 190.1 %shard_map.118 = bf16[512,8192]{1,0:T(8,128)(2,1)} custom-call(s32[1]{0:T(128)S(6)} %copy.14.len_ref, bf16[512,8192]{1,0:T(8,128)(2,1)} %bitcast.7, f32[1,8192]{1,0:T(1,128)} %bitcast.8, f32[64,8192]{1,0:T(8,128)} %wq.1, f32[64,1024]{1,0:T(8,128)} %wk.1, f32[64,1024]{1,0:T(8,128)} %wv.1, f32[64,8192]{1,0:T(8,128)} %wo.1, f32[64,128]{1,0:T(8,128)} %bitcast.9, ...), custom_call_target="tpu_custom_call" | custom-call | tf_op jit(solution)/shard_map/pallas_call | solution.py:625
  190.8 7.8 %copy.15 = bf16[1,512,8192]{2,1,0:T(8,128)(2,1)} copy(bf16[1,512,8192]{2,1,0:T(8,128)(2,1)} %bitcast.6) | data formatting | bytes 16777216

commit v3 on v2

--- a/solution.py
+++ b/solution.py
@@ -26,15 +26,17 @@
 QT = 64
 KT = 8
 Q_CHUNKS = 8
-Q_FIRST = 3
+Q_FIRST = 1
 O_CHUNKS = 4
 O_FIRST = 2
+O_EARLY = 2
+O_MID = 3
 G_FIRST = 2
 
 
 def kernel(
-    len_ref, hid_hbm, gain, wq, wk, wv, wo, bq, bk, bv, cos, sin, out,
-    wf, pm, pk_own, pk_oth, sc, hid, send_a, wbuf, send_o, wobuf, acc, qb, kv_own, kv_oth, att, acc2, outb,
+    len_ref, hid_hbm, gain_hbm, wq, wk, wv, wo, bq_hbm, bk_hbm, bv_hbm, cos_hbm, sin_hbm, out,
+    gain, bq, bk, bv, cos, sin, wf, pm, pk_own, pk_oth, sc, hid, send_a, wbuf, send_o, wobuf, acc, qb, kv_own, kv_oth, att, acc2, outb,
     ld_sem, pk_sem, a_send, a_recv, b_send, b_recv, sib_sem, o_send, o_recv, kv_sem, t_send, t_recv, g_send, g_recv, g_loc,
 ):
     dp = lax.axis_index("dp")
@@ -68,6 +70,12 @@
         pltpu.make_async_copy(wv, wf.at[:, 9216:10240], ld_sem.at[2]),
         pltpu.make_async_copy(wo, wf.at[:, 10240:18432], ld_sem.at[3]),
         pltpu.make_async_copy(hid_hbm, hid, ld_sem.at[4]),
+        pltpu.make_async_copy(gain_hbm, gain, ld_sem.at[5]),
+        pltpu.make_async_copy(bq_hbm, bq, ld_sem.at[6]),
+        pltpu.make_async_copy(bk_hbm, bk, ld_sem.at[7]),
+        pltpu.make_async_copy(bv_hbm, bv, ld_sem.at[8]),
+        pltpu.make_async_copy(cos_hbm, cos, ld_sem.at[9]),
+        pltpu.make_async_copy(sin_hbm, sin, ld_sem.at[10]),
     )
     for cp in loads:
         cp.start()
@@ -145,7 +153,8 @@
     def _():
         remote(send_o, wobuf.at[half_rows], sib_sem.at[1], sib_sem.at[2], dev_sib).start()
 
-    loads[4].wait()
+    for cp in loads[4:]:
+        cp.wait()
 
     @pl.loop(0, 32)
     def _(i):
@@ -211,6 +220,16 @@
             else:
                 acc[...] += part
 
+    @pl.when(source)
+    def _():
+        pltpu.make_async_copy(send_o, wobuf.at[half_rows], sib_sem.at[0]).wait()
+        remote(send_o, wobuf.at[half_rows], sib_sem.at[1], sib_sem.at[2], dev_sib).wait_recv()
+
+        @pl.loop(0, O_EARLY)
+        def _(k):
+            o_copy(0, slot, k, 4 * k, dev_yu, 0).start()
+            o_copy(0, slot, k, 4 * k + 1, dev_yd, 0).start()
+
     @pl.loop(0, Q_CHUNKS)
     def _(j):
         @pl.loop(0, 2)
@@ -226,9 +245,6 @@
 
     @pl.when(source)
     def _():
-        pltpu.make_async_copy(send_o, wobuf.at[half_rows], sib_sem.at[0]).wait()
-        remote(send_o, wobuf.at[half_rows], sib_sem.at[1], sib_sem.at[2], dev_sib).wait_recv()
-
         @pl.loop(0, O_FIRST)
         def _(k):
             o_copy(0, slot, k, 4 * k + 2, dev_xp, 1).start()
@@ -267,7 +283,7 @@
 
     @pl.when(source)
     def _():
-        @pl.loop(0, O_CHUNKS)
+        @pl.loop(O_EARLY, O_CHUNKS)
         def _(k):
             o_copy(0, slot, k, 4 * k, dev_yu, 0).start()
             o_copy(0, slot, k, 4 * k + 1, dev_yd, 0).start()
@@ -277,6 +293,23 @@
             o_wait(1, slot, k)
             o_copy(1, slot, k, 16 + 2 * k, dev_yu, 1).start()
             o_copy(1, slot, k, 17 + 2 * k, dev_yd, 1).start()
+
+    def o_pass(k):
+        o_wait(0, s_dn, k)
+        o_wait(0, s_up, k)
+
+        @pl.when(k >= O_FIRST)
+        def _():
+            o_copy(0, s_dn, k, 4 * k + 1, dev_xp, 1).start()
+            o_copy(0, s_up, k, 4 * k + 2, dev_xp, 1).start()
+
+        o_forward(0, k, 4 * k)
+
+    @pl.when(jnp.logical_not(source))
+    def _():
+        @pl.loop(0, O_EARLY)
+        def _(k):
+            o_pass(k)
 
     project(0, y_dn)
     project(0, y_up)
@@ -320,6 +353,18 @@
     kv_swap = remote(kv_own, kv_oth, kv_sem.at[0], kv_sem.at[1], dev_kv)
     kv_swap.start()
 
+    @pl.when(source)
+    def _():
+        @pl.loop(O_FIRST, O_CHUNKS)
+        def _(k):
+            o_copy(0, slot, k, 4 * k + 2, dev_xp, 1).start()
+
+    @pl.when(jnp.logical_not(source))
+    def _():
+        @pl.loop(O_EARLY, O_MID)
+        def _(k):
+            o_pass(k)
+
     for h in range(4):
         cols = slice(h * 128, (h + 1) * 128)
         raw_q = acc[:, cols] + bq[pl.ds(g_me * 4 + h, 1), :]
@@ -345,22 +390,23 @@
     def tid(xh_, z_, c_):
         return xh_ * 8 + z_ * 2 + c_
 
+    def gather_cross(copy, wait, chunks, first):
+        own = tid(1 - xh, z, c)
+
+        @pl.loop(0, chunks)
+        def _(h):
+            wait(own, h)
+
+            @pl.when(h < first)
+            def _():
+                copy(own, h, 15 * h + 8, dev_zu).start()
+                copy(own, h, 15 * h + 9, dev_zd).start()
+
+            copy(own, h, 15 * h + 10, dev_sib).start()
+
     def gather_side(copy, wait, chunks, first, side):
         xs = (xh + side) % 2
-        own, dn, up = tid(xs, z, c), tid(xs, z_dn, c), tid(xs, z_up, c)
-        if side == 1:
-
-            @pl.loop(0, chunks)
-            def _(h):
-                wait(own, h)
-
-                @pl.when(h < first)
-                def _():
-                    copy(own, h, 15 * h + 8, dev_zu).start()
-                    copy(own, h, 15 * h + 9, dev_zd).start()
-
-                copy(own, h, 15 * h + 10, dev_sib).start()
-
+        dn, up = tid(xs, z_dn, c), tid(xs, z_up, c)
         @pl.loop(0, chunks)
         def _(h):
             n = 15 * h + 4 + 7 * side
@@ -433,25 +479,14 @@
 
         start_own(t_copy, n)
 
-    @pl.when(source)
-    def _():
-        @pl.loop(O_FIRST, O_CHUNKS)
-        def _(k):
-            o_copy(0, slot, k, 4 * k + 2, dev_xp, 1).start()
-
     @pl.when(jnp.logical_not(source))
     def _():
-        @pl.loop(0, O_CHUNKS)
+        @pl.loop(O_MID, O_CHUNKS)
         def _(k):
             o_wait(0, s_dn, k)
             o_wait(0, s_up, k)
             o_forward(0, k, 4 * k)
 
-            @pl.when(k >= O_FIRST)
-            def _():
-                o_copy(0, s_dn, k, 4 * k + 1, dev_xp, 1).start()
-                o_copy(0, s_up, k, 4 * k + 2, dev_xp, 1).start()
-
         @pl.loop(0, O_FIRST)
         def _(k):
             o_wait(1, s_dn, k)
@@ -459,6 +494,7 @@
             o_forward(1, k, 4 * k + 1)
 
     gather_side(t_copy, t_wait, 2, 2, 0)
+    gather_cross(t_copy, t_wait, 2, 2)
 
     @pl.when(source)
     def _():
@@ -469,6 +505,13 @@
             @pl.when(k >= O_FIRST)
             def _():
                 o_copy(0, 1 - slot, k, 4 * k + 3, dev_xp, 1).start()
+
+    @pl.when(jnp.logical_not(source))
+    def _():
+        @pl.loop(O_MID, O_CHUNKS)
+        def _(k):
+            o_copy(0, s_dn, k, 4 * k + 1, dev_xp, 1).start()
+            o_copy(0, s_up, k, 4 * k + 2, dev_xp, 1).start()
 
     gather_side(t_copy, t_wait, 2, 2, 1)
     gather_last(t_copy, t_wait, 2, 2, 0)
@@ -553,6 +596,7 @@
 
     gather_side(g_copy, g_wait, 4, G_FIRST, 0)
     gather_last(g_copy, g_wait, 4, G_FIRST, 0)
+    gather_cross(g_copy, g_wait, 4, G_FIRST)
     gather_side(g_copy, g_wait, 4, G_FIRST, 1)
     gather_last(g_copy, g_wait, 4, G_FIRST, 1)
     wait_sibling(g_wait, 4)
@@ -619,17 +663,21 @@
     cos = np.concatenate((cosine, cosine), axis=1).astype(np.float32)
     sin = np.concatenate((-sine, sine), axis=1).astype(np.float32)
     anywhere = pl.BlockSpec(memory_space=pl.ANY)
-    vmem = pl.BlockSpec(memory_space=pltpu.VMEM)
+    hbm = pl.BlockSpec(memory_space=pltpu.HBM)
     bf, f32 = jnp.bfloat16, jnp.float32
     dma = pltpu.SemaphoreType.DMA
     result = pl.pallas_call(
         kernel,
         out_shape=jax.ShapeDtypeStruct((TOK, D), bf),
-        in_specs=[pl.BlockSpec(memory_space=pltpu.SMEM), anywhere, vmem]
-        + [anywhere] * 4
-        + [vmem] * 5,
+        in_specs=[pl.BlockSpec(memory_space=pltpu.SMEM)] + [hbm] * 11,
         out_specs=anywhere,
         scratch_shapes=[
+            pltpu.VMEM((1, D), f32),
+            pltpu.VMEM((HQ, HD), f32),
+            pltpu.VMEM((KV, HD), f32),
+            pltpu.VMEM((KV, HD), f32),
+            pltpu.VMEM((TOK, HD), f32),
+            pltpu.VMEM((TOK, HD), f32),
             pltpu.VMEM((ROWS, 18432), f32),
             pltpu.VMEM((144, 8, 128), f32),
             pltpu.VMEM((144, 128), f32),
@@ -647,7 +695,7 @@
             pltpu.VMEM((GROUPS, TOK, GCOLS), bf),
             pltpu.VMEM((TOK, GCOLS), f32),
             pltpu.VMEM((4, TOK, 128), bf),
-            dma((5,)),
+            dma((11,)),
             dma((2,)),
             dma((16,)),
             dma((16,)),

time: 199 us -> 187 us (0.940)
  Pallas kernels: 190 us -> 178 us
    pallas_call x1, Pallas kernels: 190 us -> 178 us  [local(): pl.pallas_call(kernel, out_shape=jax.ShapeDtypeStruct((TOK, D), bf), in_s...]
where the time goes in v3:
time: 187 us
  Pallas kernels  178 us (95%)
  local copies, waits for them, and re-layouts  7.77 us (4%)
    pallas_call x1, Pallas kernels, local(): pl.pallas_call(kernel, out_shape=jax.ShapeDtypeStruct((TOK, D), bf), in_s...  178 us
    unnamed x1, local copies, waits for them, and re-layouts  7.77 us

profile of v3, /device:TPU:27, one launch (start us, length us, event | category | flops | bytes accessed | tf_op | source)
XLA Modules:
  0.0 186.8 jit_solution(16007869986817117717)
XLA Ops:
  0.7 178.4 %shard_map.118 = bf16[512,8192]{1,0:T(8,128)(2,1)} custom-call(s32[1]{0:T(128)S(6)} %copy.14.len_ref, bf16[512,8192]{1,0:T(8,128)(2,1)} %bitcast.7, f32[1,8192]{1,0:T(1,128)} %bitcast.8, f32[64,8192]{1,0:T(8,128)} %wq.1, f32[64,1024]{1,0:T(8,128)} %wk.1, f32[64,1024]{1,0:T(8,128)} %wv.1, f32[64,8192]{1,0:T(8,128)} %wo.1, f32[64,128]{1,0:T(8,128)} %bitcast.9, ...), custom_call_target="tpu_custom_call" | custom-call | tf_op jit(solution)/shard_map/pallas_call | solution.py:669
  179.1 7.8 %copy.15 = bf16[1,512,8192]{2,1,0:T(8,128)(2,1)} copy(bf16[1,512,8192]{2,1,0:T(8,128)(2,1)} %bitcast.6) | data formatting | bytes 16777216

commit v4 on v3

--- a/solution.py
+++ b/solution.py
@@ -27,11 +27,15 @@
 KT = 8
 Q_CHUNKS = 8
 Q_FIRST = 1
-O_CHUNKS = 4
-O_FIRST = 2
-O_EARLY = 2
-O_MID = 3
-G_FIRST = 2
+O_CHUNKS = 8
+O_ROWS = 16
+O_FIRST = 4
+O_EARLY = 0
+O_MID = 6
+T_CHUNKS = 4
+T_ROWS = 128
+G_CHUNKS = 8
+G_FIRST = 4
 
 
 def kernel(
@@ -164,7 +168,7 @@
         hid[rows, :] = (wide * lax.rsqrt(ms + NORM_EPS) * gain[...]).astype(jnp.bfloat16)
 
     def o_rows(side, s, k):
-        return pl.ds(pl.multiple_of(side * 256 + s * 128 + k * 32, 32), 32)
+        return pl.ds(pl.multiple_of(side * 256 + s * 128 + k * O_ROWS, O_ROWS), O_ROWS)
 
     def o_copy(side, s, k, n, device, to_side):
         return remote(
@@ -243,12 +247,6 @@
         b_copy(0, y, j, 3 * j + 1, dev_yu, 0).start()
         b_copy(0, y, j, 3 * j + 2, dev_yd, 0).start()
 
-    @pl.when(source)
-    def _():
-        @pl.loop(0, O_FIRST)
-        def _(k):
-            o_copy(0, slot, k, 4 * k + 2, dev_xp, 1).start()
-
     @pl.loop(0, Q_FIRST)
     def _(j):
         n = 24 + 4 * j
@@ -283,16 +281,16 @@
 
     @pl.when(source)
     def _():
+        @pl.loop(0, O_FIRST)
+        def _(k):
+            o_copy(0, slot, k, 4 * k + 2, dev_xp, 1).start()
+
+    @pl.when(source)
+    def _():
         @pl.loop(O_EARLY, O_CHUNKS)
         def _(k):
             o_copy(0, slot, k, 4 * k, dev_yu, 0).start()
             o_copy(0, slot, k, 4 * k + 1, dev_yd, 0).start()
-
-        @pl.loop(0, O_FIRST)
-        def _(k):
-            o_wait(1, slot, k)
-            o_copy(1, slot, k, 16 + 2 * k, dev_yu, 1).start()
-            o_copy(1, slot, k, 17 + 2 * k, dev_yd, 1).start()
 
     def o_pass(k):
         o_wait(0, s_dn, k)
@@ -377,7 +375,7 @@
     kv_oth[...] = values
 
     def t_ref(src_t, h):
-        return att.at[group_of(src_t), pl.ds(pl.multiple_of(h * 256, 256), 256)]
+        return att.at[group_of(src_t), pl.ds(pl.multiple_of(h * T_ROWS, T_ROWS), T_ROWS)]
 
     def t_copy(src_t, h, n, device):
         ref = t_ref(src_t, h)
@@ -477,7 +475,16 @@
             o = jnp.dot(p, kv_oth[0:hi, :], preferred_element_type=jnp.float32)
             att[g_me, lo:hi, cols] = o.astype(jnp.bfloat16)
 
-        start_own(t_copy, n)
+        start_own(t_copy, 2 * n)
+        start_own(t_copy, 2 * n + 1)
+
+    @pl.when(source)
+    def _():
+        @pl.loop(0, O_FIRST)
+        def _(k):
+            o_wait(1, slot, k)
+            o_copy(1, slot, k, 4 * O_CHUNKS + 2 * k, dev_yu, 1).start()
+            o_copy(1, slot, k, 4 * O_CHUNKS + 2 * k + 1, dev_yd, 1).start()
 
     @pl.when(jnp.logical_not(source))
     def _():
@@ -487,86 +494,36 @@
             o_wait(0, s_up, k)
             o_forward(0, k, 4 * k)
 
+    gather_side(t_copy, t_wait, T_CHUNKS, T_CHUNKS, 0)
+    gather_cross(t_copy, t_wait, T_CHUNKS, T_CHUNKS)
+
+    @pl.when(source)
+    def _():
+        @pl.loop(0, O_CHUNKS)
+        def _(k):
+            o_wait(0, 1 - slot, k)
+
+            @pl.when(k >= O_FIRST)
+            def _():
+                o_copy(0, 1 - slot, k, 4 * k + 3, dev_xp, 1).start()
+
+    @pl.when(jnp.logical_not(source))
+    def _():
+        @pl.loop(O_MID, O_CHUNKS)
+        def _(k):
+            o_copy(0, s_dn, k, 4 * k + 1, dev_xp, 1).start()
+            o_copy(0, s_up, k, 4 * k + 2, dev_xp, 1).start()
+
+    @pl.when(jnp.logical_not(source))
+    def _():
         @pl.loop(0, O_FIRST)
         def _(k):
             o_wait(1, s_dn, k)
             o_wait(1, s_up, k)
             o_forward(1, k, 4 * k + 1)
 
-    gather_side(t_copy, t_wait, 2, 2, 0)
-    gather_cross(t_copy, t_wait, 2, 2)
-
-    @pl.when(source)
-    def _():
-        @pl.loop(0, O_CHUNKS)
-        def _(k):
-            o_wait(0, 1 - slot, k)
-
-            @pl.when(k >= O_FIRST)
-            def _():
-                o_copy(0, 1 - slot, k, 4 * k + 3, dev_xp, 1).start()
-
-    @pl.when(jnp.logical_not(source))
-    def _():
-        @pl.loop(O_MID, O_CHUNKS)
-        def _(k):
-            o_copy(0, s_dn, k, 4 * k + 1, dev_xp, 1).start()
-            o_copy(0, s_up, k, 4 * k + 2, dev_xp, 1).start()
-
-    gather_side(t_copy, t_wait, 2, 2, 1)
-    gather_last(t_copy, t_wait, 2, 2, 0)
-
-    @pl.when(source)
-    def _():
-        @pl.loop(O_FIRST, O_CHUNKS)
-        def _(k):
-            o_wait(1, slot, k)
-
-        @pl.loop(0, O_CHUNKS)
-        def _(k):
-            o_wait(1, 1 - slot, k)
-
-    @pl.when(jnp.logical_not(source))
-    def _():
-        @pl.loop(O_FIRST, O_CHUNKS)
-        def _(k):
-            o_wait(1, s_dn, k)
-            o_wait(1, s_up, k)
-
-    def add_group(src_t, first=False):
-        g = group_of(src_t)
-        part = lax.dot_general(
-            att[g],
-            wobuf[:, pl.ds(pl.multiple_of(g * 512, 512), 512)],
-            (((1,), (1,)), ((), ())),
-            preferred_element_type=jnp.float32,
-        )
-        if first:
-            acc2[...] = part
-        else:
-            acc2[...] += part
-
-    def near(i):
-        step = i % 4
-        return (xh + i // 4) % 2, (z + ring(step)) % 4
-
-    add_group(t, True)
-
-    @pl.loop(1, 7)
-    def _(i):
-        xs, zs = near(i)
-        add_group(tid(xs, zs, c))
-
-    gather_last(t_copy, t_wait, 2, 2, 1)
-    add_group(tid(1 - xh, z_op, c))
-
-    @pl.loop(0, 8)
-    def _(i):
-        xs, zs = near(i)
-        src = tid(xs, zs, 1 - c)
-        t_wait(src, 0)
-        t_wait(src, 1)
-        add_group(src)
+    gather_side(t_copy, t_wait, T_CHUNKS, T_CHUNKS, 1)
+    gather_last(t_copy, t_wait, T_CHUNKS, T_CHUNKS, 0)
 
     def out_block(src_t, j):
         xh_s, z_s, c_s = src_t // 8, (src_t // 2) % 4, src_t % 2
@@ -576,7 +533,8 @@
         return (xl_b * 4 + c_s + 2 * s) * 8 + xh_b * 4 + z_s
 
     def g_ref(src_t, j):
-        return out.at[:, pl.ds(pl.multiple_of(out_block(src_t, j) * 128, 128), 128)]
+        col = out_block(src_t, j // 2) * 128
+        return out.at[pl.ds(pl.multiple_of((j % 2) * 256, 256), 256), pl.ds(pl.multiple_of(col, 128), 128)]
 
     def g_copy_own(src_t, j, n, device):
         return remote(outb.at[j], g_ref(src_t, j), g_send.at[n], g_recv.at[src_t, j], device)
@@ -589,19 +547,87 @@
         ref = g_ref(src_t, j)
         remote(ref, ref, g_send.at[0], g_recv.at[src_t, j], dev_sib).wait_recv()
 
-    for j in range(4):
-        outb[j] = acc2[:, j * 128 : (j + 1) * 128].astype(jnp.bfloat16)
-        pltpu.make_async_copy(outb.at[j], g_ref(t, j), g_loc.at[j]).start()
-        start_own(g_copy_own, j)
-
-    gather_side(g_copy, g_wait, 4, G_FIRST, 0)
-    gather_last(g_copy, g_wait, 4, G_FIRST, 0)
-    gather_cross(g_copy, g_wait, 4, G_FIRST)
-    gather_side(g_copy, g_wait, 4, G_FIRST, 1)
-    gather_last(g_copy, g_wait, 4, G_FIRST, 1)
-    wait_sibling(g_wait, 4)
-
-    for j in range(4):
+    def near(i):
+        return (xh + i // 4) % 2, (z + ring(i % 4)) % 4
+
+    def sibling_wait(i):
+        xs, zs = near(i)
+
+        @pl.loop(0, T_CHUNKS)
+        def _(h):
+            t_wait(tid(xs, zs, 1 - c), h)
+
+    def add_pair(i, half, first=False):
+        xs, zs = near(i)
+        parts = []
+        for core in range(2):
+            g = group_of(tid(xs, zs, core))
+            parts.append(
+                lax.dot_general(
+                    att[g],
+                    wobuf[half * 256 : (half + 1) * 256, pl.ds(pl.multiple_of(g * 512, 512), 512)],
+                    (((1,), (1,)), ((), ())),
+                    preferred_element_type=jnp.float32,
+                )
+            )
+        if first:
+            acc2[...] = parts[0] + parts[1]
+        else:
+            acc2[...] += parts[0] + parts[1]
+
+    def send_half(half):
+        for n in range(4):
+            j = half * 4 + n
+            rows, cols = slice((n % 2) * 256, (n % 2 + 1) * 256), slice((n // 2) * 128, (n // 2 + 1) * 128)
+            outb[j] = acc2[rows, cols].astype(jnp.bfloat16)
+            pltpu.make_async_copy(outb.at[j], g_ref(t, j), g_loc.at[j]).start()
+            start_own(g_copy_own, j)
+
+    sibling_wait(0)
+    add_pair(0, 0, True)
+
+    @pl.loop(1, 7)
+    def _(i):
+        sibling_wait(i)
+        add_pair(i, 0)
+
+    gather_last(t_copy, t_wait, T_CHUNKS, T_CHUNKS, 1)
+    sibling_wait(7)
+    add_pair(7, 0)
+    send_half(0)
+
+    @pl.when(source)
+    def _():
+        @pl.loop(O_FIRST, O_CHUNKS)
+        def _(k):
+            o_wait(1, slot, k)
+
+        @pl.loop(0, O_CHUNKS)
+        def _(k):
+            o_wait(1, 1 - slot, k)
+
+    @pl.when(jnp.logical_not(source))
+    def _():
+        @pl.loop(O_FIRST, O_CHUNKS)
+        def _(k):
+            o_wait(1, s_dn, k)
+            o_wait(1, s_up, k)
+
+    add_pair(0, 1, True)
+
+    @pl.loop(1, 8)
+    def _(i):
+        add_pair(i, 1)
+
+    send_half(1)
+    gather_side(g_copy, g_wait, G_CHUNKS, G_FIRST, 0)
+    gather_last(g_copy, g_wait, G_CHUNKS, G_FIRST, 0)
+    gather_cross(g_copy, g_wait, G_CHUNKS, G_FIRST)
+    gather_side(g_copy, g_wait, G_CHUNKS, G_FIRST, 1)
+    gather_last(g_copy, g_wait, G_CHUNKS, G_FIRST, 1)
+    wait_sibling(g_wait, G_CHUNKS)
+
+    for j in range(G_CHUNKS):
         pltpu.make_async_copy(outb.at[j], g_ref(t, j), g_loc.at[j]).wait()
 
     def drain(ref, sem):
@@ -624,33 +650,33 @@
         @pl.loop(0, O_CHUNKS)
         def _(k):
             for n in range(3):
-                drain(wobuf.at[0:32], o_send.at[4 * k + n])
+                drain(wobuf.at[0:O_ROWS], o_send.at[4 * k + n])
 
             @pl.when(k >= O_FIRST)
             def _():
-                drain(wobuf.at[0:32], o_send.at[4 * k + 3])
+                drain(wobuf.at[0:O_ROWS], o_send.at[4 * k + 3])
 
             @pl.when(k < O_FIRST)
             def _():
-                drain(wobuf.at[0:32], o_send.at[16 + 2 * k])
-                drain(wobuf.at[0:32], o_send.at[17 + 2 * k])
+                drain(wobuf.at[0:O_ROWS], o_send.at[4 * O_CHUNKS + 2 * k])
+                drain(wobuf.at[0:O_ROWS], o_send.at[4 * O_CHUNKS + 2 * k + 1])
 
     @pl.when(jnp.logical_not(source))
     def _():
         @pl.loop(0, O_CHUNKS)
         def _(k):
-            drain(wobuf.at[0:32], o_send.at[4 * k])
-            drain(wobuf.at[0:32], o_send.at[4 * k + 1])
+            drain(wobuf.at[0:O_ROWS], o_send.at[4 * k])
+            drain(wobuf.at[0:O_ROWS], o_send.at[4 * k + 1])
 
             @pl.when(k >= O_FIRST)
             def _():
-                drain(wobuf.at[0:32], o_send.at[4 * k + 2])
-
-    @pl.loop(0, 30)
+                drain(wobuf.at[0:O_ROWS], o_send.at[4 * k + 2])
+
+    @pl.loop(0, 15 * T_CHUNKS)
     def _(n):
-        drain(att.at[0, 0:256], t_send.at[n])
-
-    @pl.loop(0, 60)
+        drain(att.at[0, 0:T_ROWS], t_send.at[n])
+
+    @pl.loop(0, 15 * G_CHUNKS)
     def _(n):
         drain(outb.at[0], g_send.at[n])
 
@@ -693,8 +719,8 @@
             pltpu.VMEM((TOK, HD), bf),
             pltpu.VMEM((TOK, HD), bf),
             pltpu.VMEM((GROUPS, TOK, GCOLS), bf),
-            pltpu.VMEM((TOK, GCOLS), f32),
-            pltpu.VMEM((4, TOK, 128), bf),
+            pltpu.VMEM((TOK, 256), f32),
+            pltpu.VMEM((G_CHUNKS, 256, 128), bf),
             dma((11,)),
             dma((2,)),
             dma((16,)),
@@ -702,14 +728,14 @@
             dma((56,)),
             dma((2, 4, Q_CHUNKS)),
             dma((3,)),
-            dma((20,)),
-            dma((2, 2, 4)),
+            dma((4 * O_CHUNKS + 2 * O_FIRST,)),
+            dma((2, 2, O_CHUNKS)),
             dma((2,)),
-            dma((30,)),
-            dma((16, 2)),
-            dma((60,)),
-            dma((16, 4)),
-            dma((4,)),
+            dma((15 * T_CHUNKS,)),
+            dma((16, T_CHUNKS)),
+            dma((15 * G_CHUNKS,)),
+            dma((16, G_CHUNKS)),
+            dma((G_CHUNKS,)),
         ],
         compiler_params=pltpu.CompilerParams(
             collective_id=0, has_side_effects=True, vmem_limit_bytes=62 * 2**20

time: 187 us -> 179 us (0.957)
  Pallas kernels: 178 us -> 170 us
    pallas_call x1, Pallas kernels: 178 us -> 170 us  [local(): pl.pallas_call(kernel, out_shape=jax.ShapeDtypeStruct((TOK, D), bf), in_s...]
where the time goes in v4:
time: 179 us; the launch traced here: 178 us
  Pallas kernels  170 us (95%)
  local copies, waits for them, and re-layouts  7.77 us (4%)
    pallas_call x1, Pallas kernels, local(): pl.pallas_call(kernel, out_shape=jax.ShapeDtypeStruct((TOK, D), bf), in_s...  170 us
    unnamed x1, local copies, waits for them, and re-layouts  7.77 us

profile of v4, /device:TPU:27, one launch (start us, length us, event | category | flops | bytes accessed | tf_op | source)
XLA Modules:
  0.0 178.1 jit_solution(9717279410579464297)
XLA Ops:
  0.7 169.6 %shard_map.118 = bf16[512,8192]{1,0:T(8,128)(2,1)} custom-call(s32[1]{0:T(128)S(6)} %copy.14.len_ref, bf16[512,8192]{1,0:T(8,128)(2,1)} %bitcast.7, f32[1,8192]{1,0:T(1,128)} %bitcast.8, f32[64,8192]{1,0:T(8,128)} %wq.1, f32[64,1024]{1,0:T(8,128)} %wk.1, f32[64,1024]{1,0:T(8,128)} %wv.1, f32[64,8192]{1,0:T(8,128)} %wo.1, f32[64,128]{1,0:T(8,128)} %bitcast.9, ...), custom_call_target="tpu_custom_call" | custom-call | tf_op jit(solution)/shard_map/pallas_call | solution.py:695
  170.3 7.8 %copy.15 = bf16[1,512,8192]{2,1,0:T(8,128)(2,1)} copy(bf16[1,512,8192]{2,1,0:T(8,128)(2,1)} %bitcast.6) | data formatting | bytes 16777216

commit v5 on v4

--- a/solution.py
+++ b/solution.py
@@ -81,7 +81,7 @@
         pltpu.make_async_copy(cos_hbm, cos, ld_sem.at[9]),
         pltpu.make_async_copy(sin_hbm, sin, ld_sem.at[10]),
     )
-    for cp in loads:
+    for cp in loads[:3]:
         cp.start()
 
     barrier = pltpu.get_barrier_semaphore()
@@ -93,23 +93,34 @@
     for peer in (dev_yu, dev_yd, dev_xp):
         pl.semaphore_signal(barrier, inc=1, device_id=peer, device_id_type=MESH)
 
-    for cp in loads[:4]:
+    def peaks(lo, hi):
+        @pl.loop(lo, hi, unroll=4)
+        def _(j):
+            tile = jnp.abs(wf[:, pl.ds(pl.multiple_of(j * 128, 128), 128)])
+            pm[j] = jnp.max(tile.reshape(8, 8, 128), axis=0)
+
+        top = jnp.max(jnp.max(pm[lo:hi], axis=1), axis=1, keepdims=True)
+        pk_own[lo:hi, :] = jnp.broadcast_to(top, (hi - lo, 128))
+
+    def swap(lo, hi, n):
+        rows = pl.ds(lo, hi - lo)
+        return remote(pk_own.at[rows], pk_oth.at[rows], pk_sem.at[n], pk_sem.at[n + 1], dev_sib)
+
+    def scales(lo, hi):
+        full = jnp.maximum(pk_own[lo:hi, :], pk_oth[lo:hi, :])
+        sc[lo:hi, :] = ((full + PEAK_EPS) / LEVEL_TOP).astype(jnp.bfloat16).astype(jnp.float32)
+
+    first_tiles = QT + 2 * KT
+    for cp in loads[:3]:
         cp.wait()
-
-    @pl.loop(0, 144, unroll=4)
-    def _(j):
-        tile = jnp.abs(wf[:, pl.ds(pl.multiple_of(j * 128, 128), 128)])
-        pm[j] = jnp.max(tile.reshape(8, 8, 128), axis=0)
-
-    peaks = jnp.max(jnp.max(pm[...], axis=1), axis=1, keepdims=True)
-    pk_own[...] = jnp.broadcast_to(peaks, (144, 128))
-
+    for cp in loads[3:]:
+        cp.start()
+    peaks(0, first_tiles)
     pl.semaphore_wait(barrier, 18)
-    swap = remote(pk_own, pk_oth, pk_sem.at[0], pk_sem.at[1], dev_sib)
-    swap.start()
-    swap.wait()
-    full = jnp.maximum(pk_own[...], pk_oth[...])
-    sc[...] = ((full + PEAK_EPS) / LEVEL_TOP).astype(jnp.bfloat16).astype(jnp.float32)
+    first_swap = swap(0, first_tiles, 0)
+    first_swap.start()
+    first_swap.wait()
+    scales(0, first_tiles)
 
     def quantized(j):
         tile = wf[:, pl.ds(pl.multiple_of(j * 128, 128), 128)]
@@ -142,6 +153,13 @@
 
     source = y % 2 == c
     slot = y // 2
+
+    loads[3].wait()
+    peaks(first_tiles, 144)
+    second_swap = swap(first_tiles, 144, 2)
+    second_swap.start()
+    second_swap.wait()
+    scales(first_tiles, 144)
 
     @pl.loop(0, 64)
     def _(j):
@@ -679,6 +697,19 @@
     @pl.loop(0, 15 * G_CHUNKS)
     def _(n):
         drain(outb.at[0], g_send.at[n])
+
+
+def hand_over(src, dst, held, in_sem, out_sem):
+    parts = [slice(n * 32, (n + 1) * 32) for n in range(16)]
+    reads = [pltpu.make_async_copy(src.at[p], held.at[p], in_sem.at[n]) for n, p in enumerate(parts)]
+    writes = [pltpu.make_async_copy(held.at[p], dst.at[p], out_sem.at[n]) for n, p in enumerate(parts)]
+    for cp in reads:
+        cp.start()
+    for read, write in zip(reads, writes):
+        read.wait()
+        write.start()
+    for cp in writes:
+        cp.wait()
 
 
 def local(hidden, lengths, norm_gain, w_q, w_k, w_v, w_out, b_q, b_k, b_v):
@@ -722,7 +753,7 @@
             pltpu.VMEM((TOK, 256), f32),
             pltpu.VMEM((G_CHUNKS, 256, 128), bf),
             dma((11,)),
-            dma((2,)),
+            dma((4,)),
             dma((16,)),
             dma((16,)),
             dma((56,)),
@@ -744,6 +775,14 @@
         lengths, hidden[0], norm_gain.reshape(1, D), w_q, w_k, w_v, w_out,
         b_q.reshape(HQ, HD), b_k.reshape(KV, HD), b_v.reshape(KV, HD), cos, sin,
     )
+    result = pl.pallas_call(
+        hand_over,
+        out_shape=jax.ShapeDtypeStruct((TOK, D), bf),
+        in_specs=[hbm],
+        out_specs=hbm,
+        scratch_shapes=[pltpu.VMEM((TOK, D), bf), dma((16,)), dma((16,))],
+        compiler_params=pltpu.CompilerParams(vmem_limit_bytes=32 * 2**20),
+    )(result)
     return result[None]
 
 

time: 179 us -> 179 us (level)
  local copies, waits for them, and re-layouts: 7.77 us -> 3.37 us
  Pallas kernels: 170 us -> 174 us
    unnamed x1 -> x2, local copies, waits for them, and re-layouts: 7.77 us -> 3.37 us
    pallas_call x0 -> x1, Pallas kernels: none -> 4.13 us  [local(): pl.pallas_call(hand_over, out_shape=jax.ShapeDtypeStruct((TOK, D), bf), i...]
where the time goes in v5:
time: 179 us; the launch traced here: 178 us
  Pallas kernels  174 us (97%)
  local copies, waits for them, and re-layouts  3.37 us (2%)
    pallas_call x1, Pallas kernels, local(): pl.pallas_call(kernel, out_shape=jax.ShapeDtypeStruct((TOK, D), bf), in_s...  170 us
    pallas_call x1, Pallas kernels, local(): pl.pallas_call(hand_over, out_shape=jax.ShapeDtypeStruct((TOK, D), bf), i...  4.13 us

profile of v5, /device:TPU:27, one launch (start us, length us, event | category | flops | bytes accessed | tf_op | source)
XLA Modules:
  0.0 177.7 jit_solution(2767287473524689739)
XLA Ops:
  0.7 169.6 %shard_map.118.src = bf16[512,8192]{1,0:T(8,128)(2,1)} custom-call(s32[1]{0:T(128)S(6)} %copy.13.len_ref, bf16[512,8192]{1,0:T(8,128)(2,1)} %bitcast.6, f32[1,8192]{1,0:T(1,128)} %bitcast.7, f32[64,8192]{1,0:T(8,128)} %wq.1, f32[64,1024]{1,0:T(8,128)} %wk.1, f32[64,1024]{1,0:T(8,128)} %wv.1, f32[64,8192]{1,0:T(8,128)} %wo.1, f32[64,128]{1,0:T(8,128)} %bitcast.8, ...), custom_call_target="tpu_custom_call" | custom-call | tf_op jit(solution)/shard_map/pallas_call | solution.py:726
  170.2 0.0 copy-start
  170.2 3.4 %copy-done = bf16[512,8192]{1,0:T(8,128)(2,1)S(1)} copy-done((bf16[512,8192]{1,0:T(8,128)(2,1)S(1)}, bf16[512,8192]{1,0:T(8,128)(2,1)}, u32[]{:S(2)}) %copy-start) | copy-done | bytes 8388632
  173.6 4.1 %shard_map.119 = bf16[512,8192]{1,0:T(8,128)(2,1)} custom-call(bf16[512,8192]{1,0:T(8,128)(2,1)S(1)} %copy-done), custom_call_target="tpu_custom_call" | custom-call | tf_op jit(solution)/shard_map/pallas_call | solution.py:778
Async XLA Ops:
  170.2 3.4 %copy-start = (bf16[512,8192]{1,0:T(8,128)(2,1)S(1)}, bf16[512,8192]{1,0:T(8,128)(2,1)}, u32[]{:S(2)}) copy-start(bf16[512,8192]{1,0:T(8,128)(2,1)} %shard_map.118.src) | copy-start | bytes 25165828
